TPU v7x, 128 devices: a whole 4x4x4 slice. The times are simulated.
128 devices in a mesh: group: 8 (over x, core), member: 16 (over y, z).
Axes of the slice: x: 4, y: 4, z: 4, core: 2. Of those that a mesh axis runs over, the one named last changes fastest.
Arguments:
- activations: bfloat16 [32768, 1152], P(('group', 'member')), may hold values from -6 to 6
- routes: int32 [32768, 1], P(('group', 'member')), may hold values from 0 to 127; in each aligned block of 256 rows (0 to 255, 256 to 511, ...) at most 4 rows name the same one
- centre_bias: float32 [1152], replicated, may hold values from -2 to 2
- centre_first: float32 [1152], replicated, may hold values from -600 to 600
- centre_second: float32 [1152], replicated, may hold values from 1000 to 1000000
- router: bfloat16 [128, 1152], P(('group', 'member')), may hold values from -0.1875 to 0.1875
- router_first: float32 [128, 1152], P(('group', 'member')), may hold values from -180 to 180
- router_second: float32 [128, 1152], P(('group', 'member')), may hold values from 100 to 100000
- encoder: bfloat16 [128, 1152, 512], P(('group', 'member')), may hold values from -0.1875 to 0.1875
- enc_bias: float32 [128, 512], P(('group', 'member')), may hold values from -3 to 3
- decoder: bfloat16 [128, 512, 1152], P(('group', 'member')), may hold values from -0.25 to 0.25
- encoder_first: float32 [128, 1152, 512], P(('group', 'member')), may hold values from -30 to 30
- encoder_second: float32 [128, 1152, 512], P(('group', 'member')), may hold values from 1 to 1000
- enc_bias_first: float32 [128, 512], P(('group', 'member')), may hold values from -60 to 60
- enc_bias_second: float32 [128, 512], P(('group', 'member')), may hold values from 10 to 10000
- decoder_first: float32 [128, 512, 1152], P(('group', 'member')), may hold values from -30 to 30
- decoder_second: float32 [128, 512, 1152], P(('group', 'member')), may hold values from 1 to 1000
Outputs:
- recon: bfloat16 [32768, 1152], P(('group', 'member'))
- new_centre: float32 [1152], replicated
- new_centre_first: float32 [1152], replicated
- new_centre_second: float32 [1152], replicated
- new_router: bfloat16 [128, 1152], P(('group', 'member'))
- new_router_first: float32 [128, 1152], P(('group', 'member'))
- new_router_second: float32 [128, 1152], P(('group', 'member'))
- new_encoder: bfloat16 [128, 1152, 512], P(('group', 'member'))
- new_enc_bias: float32 [128, 512], P(('group', 'member'))
- new_decoder: bfloat16 [128, 512, 1152], P(('group', 'member'))
- new_encoder_first: float32 [128, 1152, 512], P(('group', 'member'))
- new_encoder_second: float32 [128, 1152, 512], P(('group', 'member'))
- new_enc_bias_first: float32 [128, 512], P(('group', 'member'))
- new_enc_bias_second: float32 [128, 512], P(('group', 'member'))
- new_decoder_first: float32 [128, 512, 1152], P(('group', 'member'))
- new_decoder_second: float32 [128, 512, 1152], P(('group', 'member'))
Inputs may be any that keep to these rules, and one draw needn't show every extreme that they name: `routes`: each row names the one expert that serves it. At most 4 rows of one device name the same expert, and in every draw some device's rows name some expert exactly 4 times.
All inputs are finite; a program needn't handle non-finite values.
Results may differ from a plain program's by a relative error of at most 0.009.
Values may be sent and summed in bfloat16 or wider, within the bound.
No kernel may reach another device: no remote copies, remote signals or barrier semaphores. Data moves between devices by JAX's collectives and lax.ppermute only.
A program may use at most 128 MiB of HBM per device.

v0:
```python
import jax
import jax.numpy as jnp
from jax import lax
from jax.sharding import PartitionSpec as P

STEP = 10


learn_rate = 0.001
beta_one = 0.9
beta_two = 0.999
adam_eps = 1e-08
sparsity = 0.1


def adam_update(weights_in, gradient, moment_one, moment_two):
    first_new = beta_one * moment_one + (1.0 - beta_one) * gradient
    second_new = beta_two * moment_two + (1.0 - beta_two) * gradient * gradient
    first_hat = first_new / (1.0 - beta_one**STEP)
    second_hat = second_new / (1.0 - beta_two**STEP)
    stepped = weights_in.astype(jnp.float32) - learn_rate * first_hat / (
        jnp.sqrt(second_hat) + adam_eps
    )
    return (stepped.astype(weights_in.dtype), first_new, second_new)


def forward_pass(in_rows, centre_bias, router_row, encoder, enc_bias, decoder):
    centred = (in_rows.astype(jnp.float32) - centre_bias).astype(jnp.bfloat16)
    preact = jnp.dot(centred, encoder, preferred_element_type=jnp.float32) + enc_bias
    positive = jnp.maximum(preact, 0.0)
    latents = (positive * positive).astype(jnp.bfloat16)
    logits = jnp.dot(in_rows, router_row, preferred_element_type=jnp.float32)
    gating = jax.nn.sigmoid(logits)
    ungated = jnp.dot(latents, decoder, preferred_element_type=jnp.float32)
    rebuilt = centre_bias + gating[:, None] * ungated
    return (centred, positive, latents, gating, ungated, rebuilt)


def backward_pass(
    in_rows, live_mask, centred, positive, latents, gating, ungated, rebuilt, encoder, decoder
):
    errors = (in_rows.astype(jnp.float32) - rebuilt) * live_mask[:, None]
    backward = (-gating[:, None] * errors).astype(jnp.bfloat16)
    decoder_grad = jnp.dot(latents.T, backward, preferred_element_type=jnp.float32)
    latent_grad = jnp.dot(backward, decoder.T, preferred_element_type=jnp.float32) + sparsity
    preact_grad = (latent_grad * 2.0 * positive * live_mask[:, None]).astype(jnp.bfloat16)
    encoder_grad = jnp.dot(centred.T, preact_grad, preferred_element_type=jnp.float32)
    bias_grad = jnp.sum(preact_grad.astype(jnp.float32), axis=0)
    logit_grad = (-jnp.sum(errors * ungated, axis=1) * gating * (1.0 - gating)).astype(jnp.bfloat16)
    router_grad = jnp.dot(logit_grad, in_rows, preferred_element_type=jnp.float32)
    centre_part = -jnp.sum(errors, axis=0) - jnp.dot(
        encoder.astype(jnp.float32), bias_grad, precision=lax.Precision.HIGHEST
    )
    return (encoder_grad, bias_grad, decoder_grad, router_grad, centre_part)


def per_device(
    activations,
    routes,
    centre_bias,
    centre_first,
    centre_second,
    router,
    router_first,
    router_second,
    encoder,
    enc_bias,
    decoder,
    encoder_first,
    encoder_second,
    enc_bias_first,
    enc_bias_second,
    decoder_first,
    decoder_second,
):
    groups = lax.axis_size("group")
    members = lax.axis_size("member")
    devices = groups * members
    row_count = activations.shape[0]
    feature_count = activations.shape[1]
    slot_cap = 2 * row_count // devices
    route_ids = routes[:, 0]
    onehot = (route_ids[:, None] == jnp.arange(devices, dtype=jnp.int32)[None, :]).astype(
        jnp.float32
    )
    earlier = (jnp.arange(row_count)[:, None] > jnp.arange(row_count)[None, :]).astype(jnp.float32)
    before = jnp.dot(earlier, onehot, precision=lax.Precision.HIGHEST)
    slot_rank = jnp.sum(before * onehot, axis=1).astype(jnp.int32)
    position = route_ids * slot_cap + slot_rank
    packed = (
        jnp.zeros((devices * slot_cap, feature_count), jnp.bfloat16).at[position].set(activations)
    )
    filled = (
        jnp.zeros((devices * slot_cap,), jnp.bfloat16)
        .at[position]
        .set(jnp.ones((row_count,), jnp.bfloat16))
    )
    arrived, arrived_mask = (
        lax.all_to_all(
            packed.reshape(devices, slot_cap, feature_count),
            ("group", "member"),
            split_axis=0,
            concat_axis=0,
            tiled=True,
        ),
        lax.all_to_all(
            filled.reshape(devices, slot_cap),
            ("group", "member"),
            split_axis=0,
            concat_axis=0,
            tiled=True,
        ),
    )
    in_rows = arrived.reshape(devices * slot_cap, feature_count)
    live_mask = arrived_mask.reshape(devices * slot_cap).astype(jnp.float32)
    centred, positive, latents, gating, ungated, rebuilt = forward_pass(
        in_rows, centre_bias, router[0], encoder[0], enc_bias[0], decoder[0]
    )
    outgoing = rebuilt.astype(jnp.bfloat16)
    returned = lax.all_to_all(
        outgoing.reshape(devices, slot_cap, feature_count),
        ("group", "member"),
        split_axis=0,
        concat_axis=0,
        tiled=True,
    )
    recon = returned.reshape(devices * slot_cap, feature_count)[position]
    encoder_grad, bias_grad, decoder_grad, router_grad, centre_part = backward_pass(
        in_rows,
        live_mask,
        centred,
        positive,
        latents,
        gating,
        ungated,
        rebuilt,
        encoder[0],
        decoder[0],
    )
    router_new = adam_update(router[0], router_grad, router_first[0], router_second[0])
    encoder_new = adam_update(encoder[0], encoder_grad, encoder_first[0], encoder_second[0])
    bias_new = adam_update(enc_bias[0], bias_grad, enc_bias_first[0], enc_bias_second[0])
    decoder_new = adam_update(decoder[0], decoder_grad, decoder_first[0], decoder_second[0])
    centre_total = lax.psum(centre_part, ("group", "member"))
    centre_new = adam_update(centre_bias, centre_total, centre_first, centre_second)
    return (
        recon,
        centre_new[0],
        centre_new[1],
        centre_new[2],
        router_new[0][None],
        router_new[1][None],
        router_new[2][None],
        encoder_new[0][None],
        bias_new[0][None],
        decoder_new[0][None],
        encoder_new[1][None],
        encoder_new[2][None],
        bias_new[1][None],
        bias_new[2][None],
        decoder_new[1][None],
        decoder_new[2][None],
    )


def solution(mesh):
    placed = (
        P(("group", "member"), None),
        P(("group", "member"), None),
        P(),
        P(),
        P(),
        P(("group", "member"), None),
        P(("group", "member"), None),
        P(("group", "member"), None),
        P(("group", "member"), None, None),
        P(("group", "member"), None),
        P(("group", "member"), None, None),
        P(("group", "member"), None, None),
        P(("group", "member"), None, None),
        P(("group", "member"), None),
        P(("group", "member"), None),
        P(("group", "member"), None, None),
        P(("group", "member"), None, None),
    )
    return jax.shard_map(
        per_device,
        mesh=mesh,
        in_specs=placed,
        out_specs=(
            P(("group", "member"), None),
            P(),
            P(),
            P(),
            P(("group", "member"), None),
            P(("group", "member"), None),
            P(("group", "member"), None),
            P(("group", "member"), None, None),
            P(("group", "member"), None),
            P(("group", "member"), None, None),
            P(("group", "member"), None, None),
            P(("group", "member"), None, None),
            P(("group", "member"), None),
            P(("group", "member"), None),
            P(("group", "member"), None, None),
            P(("group", "member"), None, None),
        ),
        check_vma=False,
    )
```

profile of v0, /device:TPU:0, one launch (start us, length us, event | category | flops | bytes accessed | tf_op | source)
XLA Modules:
  0.0 155.2 jit_solution(11660463127143377981)
XLA Ops:
  0.6 1.0 fusion.22
  1.6 0.7 compare_select_fusion
  2.3 2.2 %scatter_custom_fusion.1 = bf16[512]{0:T(512)(128)(2,1)S(1)} fusion(s32[256]{0:T(256)S(1)} %bitcast.81, bf16[256]{0:T(256)(128)(2,1)S(1)} %broadcast.120, bf16[]{:T(256)} %constant.17.clone.1), kind=kCustom, calls=%fused_computation.76 | custom fusion | bytes 1026 | tf_op jit(solution)/shard_map/scatter | solution.py:96
  4.5 0.8 all_to_all.16
  5.3 11.1 %all-to-all-start.2 = ((bf16[128,1,4]{2,1,0:T(2,128)(2,1)}), bf16[128,1,4]{2,1,0:T(2,128)(2,1)S(1)}, u32[]{:S(2)}, u32[]{:S(2)}) async-start(bf16[128,1,4]{2,1,0:T(2,128)(2,1)} %all_to_all.16), calls=%async_computation.2 | async-start | bytes 131072 | tf_op jit(solution)/shard_map/all_to_all | solution.py:106
  16.4 2.6 %scatter_custom_fusion = bf16[512,1152]{1,0:T(8,128)(2,1)S(1)} fusion(s32[256]{0:T(256)S(1)} %bitcast.82, bf16[256,1152]{1,0:T(8,128)(2,1)} %param.17, bf16[]{:T(256)} %constant.17.clone.1), kind=kCustom, calls=%fused_computation.48 | custom fusion | bytes 1180160 | tf_op jit(solution)/shard_map/scatter | solution.py:91
  19.0 0.0 copy-start.3
  19.0 0.0 copy-start.9
  19.1 0.0 copy-start.10
  19.1 0.0 copy-start.1
  19.1 1.2 reshape.104
  20.2 5.6 %all-to-all-done.2 = bf16[128,1,4]{2,1,0:T(2,128)(2,1)S(1)} async-done(((bf16[128,1,4]{2,1,0:T(2,128)(2,1)}), bf16[128,1,4]{2,1,0:T(2,128)(2,1)S(1)}, u32[]{:S(2)}, u32[]{:S(2)}) %all-to-all-start.2) | async-done | bytes 1056 | tf_op jit(solution)/shard_map/all_to_all | solution.py:106
  25.8 4.6 %all-to-all-start = ((bf16[128,4,1152]{2,1,0:T(4,128)(2,1)}), bf16[128,4,1152]{2,1,0:T(4,128)(2,1)S(1)}, u32[]{:S(2)}, u32[]{:S(2)}) async-start(bf16[128,4,1152]{2,1,0:T(4,128)(2,1)} %reshape.104), calls=%async_computation | async-start | bytes 2359296 | tf_op jit(solution)/shard_map/all_to_all | solution.py:99
  30.5 0.0 copy-done.3
  30.5 0.6 reduce.2
  31.1 0.6 pad_clamp_fusion
  31.7 0.0 copy-done.9
  31.7 0.6 multiply_reduce_fusion.1
  32.3 0.2 convert_reduce_fusion.1
  32.5 0.7 reshape.108
  33.2 17.7 %all-to-all-done = bf16[128,4,1152]{2,1,0:T(4,128)(2,1)S(1)} async-done(((bf16[128,4,1152]{2,1,0:T(4,128)(2,1)}), bf16[128,4,1152]{2,1,0:T(4,128)(2,1)S(1)}, u32[]{:S(2)}, u32[]{:S(2)}) %all-to-all-start) | async-done | bytes 1179680 | tf_op jit(solution)/shard_map/all_to_all | solution.py:99
  50.9 0.5 subtract_convert_fusion.2
  51.3 1.2 convert_element_type.81
  52.5 0.3 reshape.105
  52.8 1.1 fusion.36
  54.0 0.0 copy-done
  54.0 0.0 copy-start.14
  54.0 0.0 copy-start.17
  54.0 2.2 %fusion.8 = f32[512,512]{1,0:T(8,128)S(1)} fusion(bf16[512,1152]{1,0:T(8,128)(2,1)} %convert_element_type.81, bf16[1,1152,512]{2,1,0:T(8,128)(2,1)S(1)} %copy-done, f32[512]{0:T(512)} %bitcast.85), kind=kOutput, calls=%fused_computation.25 | convolution fusion | flops 604504064 | bytes 3409920 | tf_op jit(solution)/shard_map/dot_general | solution.py:29
  56.2 0.0 copy-start.19
  56.3 0.0 copy-start.2
  56.3 0.0 copy-start.4
  56.3 1.3 multiply_reduce_fusion
  57.6 0.3 convolution_reduce_fusion
  57.9 0.0 copy-done.2
  57.9 0.0 copy-done.4
  57.9 0.6 broadcast_in_dim.54
  58.6 0.6 broadcast_in_dim.55
  59.2 0.6 broadcast_in_dim.56
  59.8 0.0 copy-done.19
  59.8 1.7 %convert_reduce_fusion = (f32[512]{0:T(512)S(1)}, bf16[512,512]{1,0:T(8,128)(2,1)}) fusion(f32[512]{0:T(512)S(1)} %copy-done.14, f32[512,512]{1,0:T(8,128)S(1)} %fusion.8, bf16[512,1152]{1,0:T(8,128)(2,1)S(1)} %get-tuple-element.35, bf16[1,512,1152]{2,1,0:T(8,128)(2,1)S(1)} %copy-done.17), kind=kOutput, calls=%fused_computation.42 | convolution fusion | flops 605814272 | bytes 3936256 | tf_op jit(solution)/shard_map/dot_general | solution.py:45
  61.5 1.0 fusion.23
  62.5 0.6 negate_subtract_fusion
  63.1 63.1 %psum.7 = f32[1152]{0:T(1024)S(1)} all-reduce(f32[1152]{0:T(1024)} %negate_subtract_fusion), channel_id=1, replica_groups=mesh['group'=8,'member'=16] {'group','member'}, use_global_device_ids=true, to_apply=%region_5.0 | all-reduce | flops 1152 | bytes 9216 | tf_op jit(solution)/shard_map/psum | solution.py:144
  126.2 1.2 reshape.106
  127.4 5.1 %all-to-all-start.1 = ((bf16[128,4,1152]{2,1,0:T(4,128)(2,1)}), bf16[128,4,1152]{2,1,0:T(4,128)(2,1)S(1)}, u32[]{:S(2)}, u32[]{:S(2)}) async-start(bf16[128,4,1152]{2,1,0:T(4,128)(2,1)} %reshape.106), calls=%async_computation.1 | async-start | bytes 2359296 | tf_op jit(solution)/shard_map/all_to_all | solution.py:120
  132.5 0.0 copy-start.6
  132.5 0.0 copy-start.11
  132.5 0.0 copy-start.12
  132.5 0.0 copy-start.13
  132.5 0.0 copy-start.7
  132.5 0.0 copy-start.8
  132.6 0.0 copy-start.15
  132.6 0.0 copy-start.16
  132.6 0.0 copy-start.20
  132.6 8.3 %fusion.28 = (f32[1,512,1152]{2,1,0:T(8,128)}, bf16[1,512,1152]{2,1,0:T(8,128)(2,1)}, f32[1,512,1152]{2,1,0:T(8,128)}) fusion(f32[1,512,1152]{2,1,0:T(8,128)} %param.33, f32[1,512,1152]{2,1,0:T(8,128)} %param.32, bf16[1,512,1152]{2,1,0:T(8,128)(2,1)} %param.27, bf16[512,1152]{1,0:T(8,128)(2,1)} %copy-done.18, f32[512,512]{1,0:T(8,128)} %copy-done.19), kind=kOutput, calls=%fused_computation.46 | convolution fusion | flops 612761600 | bytes 14024704 | tf_op jit(solution)/shard_map/dot_general | solution.py:44
  140.9 0.0 copy-done.13
  140.9 0.6 divide_subtract_fusion.1
  141.6 0.0 copy-done.8
  141.6 0.6 divide_subtract_fusion
  142.2 4.8 %fusion.29 = (f32[1,1152,512]{2,1,0:T(8,128)}, bf16[1,1152,512]{2,1,0:T(8,128)(2,1)}, f32[1,1152,512]{2,1,0:T(8,128)}) fusion(f32[1,1152,512]{2,1,0:T(8,128)S(1)} %copy-done.15, f32[1,1152,512]{2,1,0:T(8,128)S(1)} %copy-done.16, bf16[1,1152,512]{2,1,0:T(8,128)(2,1)S(1)} %copy-done, bf16[512,512]{1,0:T(8,128)(2,1)S(1)} %copy-done.20, ...), kind=kOutput, calls=%fused_computation.47 | convolution fusion | flops 614006784 | bytes 13505024 | tf_op jit(solution)/shard_map/dot_general | solution.py:47
  147.0 5.7 %all-to-all-done.1 = bf16[128,4,1152]{2,1,0:T(4,128)(2,1)S(1)} async-done(((bf16[128,4,1152]{2,1,0:T(4,128)(2,1)}), bf16[128,4,1152]{2,1,0:T(4,128)(2,1)S(1)}, u32[]{:S(2)}, u32[]{:S(2)}) %all-to-all-start.1) | async-done | bytes 1179680 | tf_op jit(solution)/shard_map/all_to_all | solution.py:120
  152.7 0.3 reshape.107
  153.0 2.2 %gather_fusion = bf16[256,1152]{1,0:T(8,128)(2,1)} fusion(bf16[512,1152]{1,0:T(8,128)(2,1)S(1)} %reshape.107, s32[1024]{0:T(1024)} %pad_clamp_fusion), kind=kCustom, calls=%fused_computation | custom fusion | bytes 1180672 | tf_op jit(solution)/shard_map/gather | solution.py:127
  (22 shorter events, 0.1 us)
Async XLA Ops:
  5.3 20.6 %all-to-all-start.2 = ((bf16[128,1,4]{2,1,0:T(2,128)(2,1)}), bf16[128,1,4]{2,1,0:T(2,128)(2,1)S(1)}, u32[]{:S(2)}, u32[]{:S(2)}) async-start(bf16[128,1,4]{2,1,0:T(2,128)(2,1)} %all_to_all.16), calls=%async_computation.2 | async-start | bytes 131072 | tf_op jit(solution)/shard_map/all_to_all | solution.py:106
  19.0 11.4 %copy-start.3 = (bf16[1,1152]{1,0:T(2,128)(2,1)S(1)}, bf16[1,1152]{1,0:T(2,128)(2,1)}, u32[]{:S(2)}) copy-start(bf16[1,1152]{1,0:T(2,128)(2,1)} %param.22) | copy-start | bytes 6916
  19.0 12.7 %copy-start.9 = (f32[1,1152]{1,0:T(1,128)S(1)}, f32[1,1152]{1,0:T(1,128)}, u32[]{:S(2)}) copy-start(f32[1,1152]{1,0:T(1,128)} %param.24) | copy-start | bytes 13828
  19.1 12.6 %copy-start.10 = (f32[1,1152]{1,0:T(1,128)S(1)}, f32[1,1152]{1,0:T(1,128)}, u32[]{:S(2)}) copy-start(f32[1,1152]{1,0:T(1,128)} %param.23) | copy-start | bytes 13828
  19.1 31.8 %copy-start.1 = (f32[1152]{0:T(1024)S(1)}, f32[1152]{0:T(1024)}, u32[]{:S(2)}) copy-start(f32[1152]{0:T(1024)} %param.19) | copy-start | bytes 13828
  25.8 25.1 %all-to-all-start = ((bf16[128,4,1152]{2,1,0:T(4,128)(2,1)}), bf16[128,4,1152]{2,1,0:T(4,128)(2,1)S(1)}, u32[]{:S(2)}, u32[]{:S(2)}) async-start(bf16[128,4,1152]{2,1,0:T(4,128)(2,1)} %reshape.104), calls=%async_computation | async-start | bytes 2359296 | tf_op jit(solution)/shard_map/all_to_all | solution.py:99
  52.5 1.5 copy-start
  54.0 2.3 %copy-start.14 = (f32[512]{0:T(512)S(1)}, f32[512]{0:T(512)}, u32[]{:S(2)}) copy-start(f32[512]{0:T(512)} %reshape.108) | copy-start | bytes 6148
  54.0 2.3 %copy-start.17 = (bf16[1,512,1152]{2,1,0:T(8,128)(2,1)S(1)}, bf16[1,512,1152]{2,1,0:T(8,128)(2,1)}, u32[]{:S(2)}) copy-start(bf16[1,512,1152]{2,1,0:T(8,128)(2,1)} %param.27) | copy-start | bytes 3538948
  56.2 3.5 %copy-start.19 = (f32[512,512]{1,0:T(8,128)}, f32[512,512]{1,0:T(8,128)S(1)}, u32[]{:S(2)}) copy-start(f32[512,512]{1,0:T(8,128)S(1)} %fusion.8) | copy-start | bytes 3145732
  56.3 1.6 %copy-start.2 = (f32[1152]{0:T(1024)S(1)}, f32[1152]{0:T(1024)}, u32[]{:S(2)}) copy-start(f32[1152]{0:T(1024)} %get-tuple-element.40) | copy-start | bytes 13828
  56.3 1.6 %copy-start.4 = (bf16[1152]{0:T(1024)(128)(2,1)S(1)}, bf16[1152]{0:T(1024)(128)(2,1)}, u32[]{:S(2)}) copy-start(bf16[1152]{0:T(1024)(128)(2,1)} %reduce.2) | copy-start | bytes 6916
  57.6 3.9 %copy-start.18 = (bf16[512,1152]{1,0:T(8,128)(2,1)}, bf16[512,1152]{1,0:T(8,128)(2,1)S(1)}, u32[]{:S(2)}) copy-start(bf16[512,1152]{1,0:T(8,128)(2,1)S(1)} %get-tuple-element.35) | copy-start | bytes 3538948
  61.5 1.0 copy-start.5
  127.4 25.3 %all-to-all-start.1 = ((bf16[128,4,1152]{2,1,0:T(4,128)(2,1)}), bf16[128,4,1152]{2,1,0:T(4,128)(2,1)S(1)}, u32[]{:S(2)}, u32[]{:S(2)}) async-start(bf16[128,4,1152]{2,1,0:T(4,128)(2,1)} %reshape.106), calls=%async_computation.1 | async-start | bytes 2359296 | tf_op jit(solution)/shard_map/all_to_all | solution.py:120
  132.5 8.4 %copy-start.6 = (f32[512]{0:T(512)S(1)}, f32[512]{0:T(512)}, u32[]{:S(2)}) copy-start(f32[512]{0:T(512)} %copy-done.5) | copy-start | bytes 6148
  132.5 8.4 %copy-start.11 = (f32[1,512]{1,0:T(1,128)S(1)}, f32[1,512]{1,0:T(1,128)}, u32[]{:S(2)}) copy-start(f32[1,512]{1,0:T(1,128)} %param.26) | copy-start | bytes 6148
  132.5 8.4 %copy-start.12 = (f32[1,512]{1,0:T(1,128)S(1)}, f32[1,512]{1,0:T(1,128)}, u32[]{:S(2)}) copy-start(f32[1,512]{1,0:T(1,128)} %param.30) | copy-start | bytes 6148
  132.5 8.4 %copy-start.13 = (f32[1,512]{1,0:T(1,128)S(1)}, f32[1,512]{1,0:T(1,128)}, u32[]{:S(2)}) copy-start(f32[1,512]{1,0:T(1,128)} %param.31) | copy-start | bytes 6148
  132.5 9.0 %copy-start.7 = (f32[1152]{0:T(1024)S(1)}, f32[1152]{0:T(1024)}, u32[]{:S(2)}) copy-start(f32[1152]{0:T(1024)} %param.20) | copy-start | bytes 13828
  132.5 9.0 %copy-start.8 = (f32[1152]{0:T(1024)S(1)}, f32[1152]{0:T(1024)}, u32[]{:S(2)}) copy-start(f32[1152]{0:T(1024)} %param.21) | copy-start | bytes 13828
  132.6 9.6 %copy-start.15 = (f32[1,1152,512]{2,1,0:T(8,128)S(1)}, f32[1,1152,512]{2,1,0:T(8,128)}, u32[]{:S(2)}) copy-start(f32[1,1152,512]{2,1,0:T(8,128)} %param.29) | copy-start | bytes 7077892
  132.6 9.6 %copy-start.16 = (f32[1,1152,512]{2,1,0:T(8,128)S(1)}, f32[1,1152,512]{2,1,0:T(8,128)}, u32[]{:S(2)}) copy-start(f32[1,1152,512]{2,1,0:T(8,128)} %param.28) | copy-start | bytes 7077892
  132.6 9.6 %copy-start.20 = (bf16[512,512]{1,0:T(8,128)(2,1)S(1)}, bf16[512,512]{1,0:T(8,128)(2,1)}, u32[]{:S(2)}) copy-start(bf16[512,512]{1,0:T(8,128)(2,1)} %get-tuple-element.38) | copy-start | bytes 1572868
where the time goes:
time: 156 us; the launch traced here: 155 us
  blocking collectives  63.1 us (40%)
  waiting for transfers between devices  29 us (19%)
  matrix products  21.8 us (14%)
  starting transfers between devices  20.9 us (13%)
  local copies, waits for them, and re-layouts  14.4 us (9%)
  other arithmetic  5.04 us (3%)
    psum x1, blocking collectives, per_device(): centre_total = lax.psum(centre_part, ('group', 'member'))  63.1 us
    all_to_all x1, waiting for transfers between devices, per_device(): lax.all_to_all(packed.reshape(devices, slot_cap, feature_count), ('group'...  17.7 us
    all_to_all x1, starting transfers between devices, per_device(): lax.all_to_all(filled.reshape(devices, slot_cap), ('group', 'member'), sp...  11.1 us
    dot_general x1, matrix products, backward_pass(): jnp.dot(latents.T, backward, preferred_element_type=jnp.float32)  8.33 us
    all_to_all x1, waiting for transfers between devices, per_device(): lax.all_to_all(outgoing.reshape(devices, slot_cap, feature_count), ('grou...  5.7 us
    all_to_all x1, waiting for transfers between devices, per_device(): lax.all_to_all(filled.reshape(devices, slot_cap), ('group', 'member'), sp...  5.58 us
    all_to_all x1, starting transfers between devices, per_device(): lax.all_to_all(outgoing.reshape(devices, slot_cap, feature_count), ('grou...  5.11 us
    dot_general x1, matrix products, backward_pass(): jnp.dot(centred.T, preact_grad, preferred_element_type=jnp.float32)  4.82 us
  transfers between devices with their start and end apart: 3, of which 3 were waited for; matrix products, arithmetic and copies ran while one was open for 13% of the time, Pallas kernels for 0%

commit v1 on v0

v1 whole, which is shorter than its diff:
```python
import jax
import jax.numpy as jnp
from jax import lax
from jax.experimental import pallas as pl
from jax.experimental.pallas import tpu as pltpu
from jax.sharding import PartitionSpec as P

STEP = 10


learn_rate = 0.001
beta_one = 0.9
beta_two = 0.999
adam_eps = 1e-08
sparsity = 0.1

AXES = ("group", "member")
EMPTY_MARK = 64.0
EMPTY_LIMIT = 32.0
VMEM_LIMIT = 48 * 1024 * 1024
NT = (((1,), (1,)), ((), ()))
TN = (((0,), (0,)), ((), ()))


def adam_update(weights_in, gradient, moment_one, moment_two):
    first_new = beta_one * moment_one + (1.0 - beta_one) * gradient
    second_new = beta_two * moment_two + (1.0 - beta_two) * gradient * gradient
    first_hat = first_new * (1.0 / (1.0 - beta_one**STEP))
    second_hat = second_new * (1.0 / (1.0 - beta_two**STEP))
    stepped = weights_in.astype(jnp.float32) - learn_rate * first_hat / (
        jnp.sqrt(second_hat) + adam_eps
    )
    return (stepped.astype(weights_in.dtype), first_new, second_new)


def slot_matrix(route_row, experts, slot_cap):
    rows = route_row.shape[1]
    onehot = lax.broadcasted_iota(jnp.int32, (experts, rows), 0) == route_row
    onehot = onehot.astype(jnp.float32)
    later = lax.broadcasted_iota(jnp.int32, (rows, rows), 0) < lax.broadcasted_iota(
        jnp.int32, (rows, rows), 1
    )
    before = jnp.dot(
        onehot.astype(jnp.bfloat16),
        later.astype(jnp.float32).astype(jnp.bfloat16),
        preferred_element_type=jnp.float32,
    )
    rank = jnp.sum(before * onehot, axis=0, keepdims=True).astype(jnp.int32)
    position = route_row * slot_cap + rank
    chosen = lax.broadcasted_iota(jnp.int32, (experts * slot_cap, rows), 0) == position
    return chosen.astype(jnp.float32)


def pack_kernel(route_ref, rows_ref, packed_ref):
    experts, slot_cap, features = packed_ref.shape
    chosen = slot_matrix(route_ref[...], experts, slot_cap)
    filled = jnp.sum(chosen, axis=1, keepdims=True)
    chosen = chosen.astype(jnp.bfloat16)
    mark = (1.0 - filled) * EMPTY_MARK
    for start in range(0, features, 128):
        part = jnp.dot(
            chosen, rows_ref[:, start : start + 128], preferred_element_type=jnp.float32
        )
        if start == 0:
            part = part + mark
        packed_ref[:, :, start : start + 128] = part.astype(jnp.bfloat16).reshape(
            experts, slot_cap, 128
        )


def unpack_kernel(route_ref, returned_ref, recon_ref):
    experts, slot_cap, wide = returned_ref.shape
    features = recon_ref.shape[1]
    chosen = slot_matrix(route_ref[...], experts, slot_cap).astype(jnp.bfloat16)
    for start in range(0, features, 128):
        block = returned_ref[:, :, start : start + 128].reshape(experts * slot_cap, 128)
        recon_ref[:, start : start + 128] = lax.dot_general(
            chosen, block, TN, preferred_element_type=jnp.float32
        ).astype(jnp.bfloat16)


def expert_kernel(
    arrived_ref,
    centre_ref,
    router_ref,
    encoder_ref,
    bias_ref,
    decoder_ref,
    outgoing_ref,
    centred_ref,
    latents_ref,
    backward_ref,
    preact_grad_ref,
    bias_grad_ref,
    router_grad_ref,
    rows_ref,
    ungated_ref,
):
    sources, slot_cap, features = arrived_ref.shape
    count = sources * slot_cap
    tail = outgoing_ref.shape[2] - features
    for start in range(0, features, 128):
        rows_ref[:, start : start + 128] = arrived_ref[:, :, start : start + 128].reshape(
            count, 128
        )
    live = rows_ref[:, 0:1].astype(jnp.float32) < EMPTY_LIMIT
    first = rows_ref[:, 0:128]
    rows_ref[:, 0:128] = jnp.where(live, first.astype(jnp.float32), 0.0).astype(jnp.bfloat16)
    live_mask = live.astype(jnp.float32)
    centre = centre_ref[...]
    centred_ref[...] = (rows_ref[...].astype(jnp.float32) - centre).astype(jnp.bfloat16)
    logits = lax.dot_general(
        rows_ref[...],
        jnp.broadcast_to(router_ref[...], (8, features)),
        NT,
        preferred_element_type=jnp.float32,
    )[:, 0:1]
    gating = jax.nn.sigmoid(logits)
    preact = (
        jnp.dot(centred_ref[...], encoder_ref[...], preferred_element_type=jnp.float32)
        + bias_ref[...]
    )
    positive = jnp.maximum(preact, 0.0)
    latents_ref[...] = (positive * positive).astype(jnp.bfloat16)
    projected = jnp.zeros((count, 1), jnp.float32)
    error_sums = []
    for start in range(0, features, 128):
        block = slice(start, start + 128)
        ungated = jnp.dot(
            latents_ref[...], decoder_ref[:, block], preferred_element_type=jnp.float32
        )
        rebuilt = centre[:, block] + gating * ungated
        outgoing_ref[:, :, block] = rebuilt.astype(jnp.bfloat16).reshape(sources, slot_cap, 128)
        errors = (rows_ref[:, block].astype(jnp.float32) - rebuilt) * live_mask
        backward_ref[:, block] = (-gating * errors).astype(jnp.bfloat16)
        projected = projected + jnp.sum(errors * ungated, axis=1, keepdims=True)
        error_sums.append(jnp.sum(errors, axis=0, keepdims=True))
    latent_grad = lax.dot_general(
        backward_ref[...], decoder_ref[...], NT, preferred_element_type=jnp.float32
    )
    preact_grad = ((latent_grad + sparsity) * 2.0 * positive * live_mask).astype(jnp.bfloat16)
    preact_grad_ref[...] = preact_grad
    bias_grad = jnp.sum(preact_grad.astype(jnp.float32), axis=0, keepdims=True)
    bias_grad_ref[...] = bias_grad
    high = bias_grad.astype(jnp.bfloat16).astype(jnp.float32)
    middle = (bias_grad - high).astype(jnp.bfloat16).astype(jnp.float32)
    low = bias_grad - high - middle
    row = lax.broadcasted_iota(jnp.int32, (8, 1), 0)
    terms = jnp.where(row == 0, high, jnp.where(row == 1, middle, jnp.where(row == 2, low, 0.0)))
    passed = jnp.sum(
        lax.dot_general(
            terms.astype(jnp.bfloat16), encoder_ref[...], NT, preferred_element_type=jnp.float32
        ),
        axis=0,
        keepdims=True,
    )
    centre_part = (-jnp.concatenate(error_sums, axis=1) - passed).astype(jnp.bfloat16)
    pieces = [centre_part[:, i * tail : (i + 1) * tail] for i in range(features // tail)]
    pieces += [jnp.zeros((1, tail), jnp.bfloat16)] * (slot_cap - len(pieces))
    tail_rows = jnp.concatenate([p.astype(jnp.float32) for p in pieces], axis=0)
    outgoing_ref[:, :, features:] = jnp.broadcast_to(
        tail_rows.astype(jnp.bfloat16)[None], (sources, slot_cap, tail)
    )
    logit_grad = (-projected * gating * (1.0 - gating)).astype(jnp.bfloat16).astype(jnp.float32)
    router_grad_ref[...] = jnp.sum(
        logit_grad * rows_ref[...].astype(jnp.float32), axis=0, keepdims=True
    )


def per_device(
    activations,
    routes,
    centre_bias,
    centre_first,
    centre_second,
    router,
    router_first,
    router_second,
    encoder,
    enc_bias,
    decoder,
    encoder_first,
    encoder_second,
    enc_bias_first,
    enc_bias_second,
    decoder_first,
    decoder_second,
):
    devices = lax.axis_size("group") * lax.axis_size("member")
    row_count, features = activations.shape
    latent_count = encoder.shape[2]
    slot_cap = 2 * row_count // devices
    count = devices * slot_cap
    wide = features + features // (slot_cap - 1)
    params = pltpu.CompilerParams(vmem_limit_bytes=VMEM_LIMIT)
    route_row = routes.reshape(1, row_count)
    packed = pl.pallas_call(
        pack_kernel,
        out_shape=jax.ShapeDtypeStruct((devices, slot_cap, features), jnp.bfloat16),
        compiler_params=params,
        name="pack",
    )(route_row, activations)
    arrived = lax.all_to_all(packed, AXES, split_axis=0, concat_axis=0, tiled=True)
    outgoing, centred, latents, backward, preact_grad, bias_grad, router_grad = pl.pallas_call(
        expert_kernel,
        out_shape=(
            jax.ShapeDtypeStruct((devices, slot_cap, wide), jnp.bfloat16),
            jax.ShapeDtypeStruct((count, features), jnp.bfloat16),
            jax.ShapeDtypeStruct((count, latent_count), jnp.bfloat16),
            jax.ShapeDtypeStruct((count, features), jnp.bfloat16),
            jax.ShapeDtypeStruct((count, latent_count), jnp.bfloat16),
            jax.ShapeDtypeStruct((1, latent_count), jnp.float32),
            jax.ShapeDtypeStruct((1, features), jnp.float32),
        ),
        scratch_shapes=[
            pltpu.VMEM((count, features), jnp.bfloat16),
            pltpu.VMEM((8, 128), jnp.float32),
        ],
        compiler_params=params,
        name="expert",
    )(arrived, centre_bias[None], router, encoder[0], enc_bias, decoder[0])
    returned = lax.all_to_all(outgoing, AXES, split_axis=0, concat_axis=0, tiled=True)
    decoder_grad = lax.dot_general(latents, backward, TN, preferred_element_type=jnp.float32)
    encoder_grad = lax.dot_general(centred, preact_grad, TN, preferred_element_type=jnp.float32)
    router_new = adam_update(router, router_grad, router_first, router_second)
    encoder_new = adam_update(encoder[0], encoder_grad, encoder_first[0], encoder_second[0])
    bias_new = adam_update(enc_bias, bias_grad, enc_bias_first, enc_bias_second)
    decoder_new = adam_update(decoder[0], decoder_grad, decoder_first[0], decoder_second[0])
    recon = pl.pallas_call(
        unpack_kernel,
        out_shape=jax.ShapeDtypeStruct((row_count, features), jnp.bfloat16),
        compiler_params=params,
        name="unpack",
    )(route_row, returned)
    centre_total = jnp.sum(
        returned[:, : slot_cap - 1, features:].astype(jnp.float32), axis=0
    ).reshape(features)
    centre_new = adam_update(centre_bias, centre_total, centre_first, centre_second)
    return (
        recon,
        centre_new[0],
        centre_new[1],
        centre_new[2],
        router_new[0],
        router_new[1],
        router_new[2],
        encoder_new[0][None],
        bias_new[0],
        decoder_new[0][None],
        encoder_new[1][None],
        encoder_new[2][None],
        bias_new[1],
        bias_new[2],
        decoder_new[1][None],
        decoder_new[2][None],
    )


def solution(mesh):
    whole, rows, blocks = P(), P(AXES, None), P(AXES, None, None)
    return jax.shard_map(
        per_device,
        mesh=mesh,
        in_specs=(
            rows, rows, whole, whole, whole, rows, rows, rows, blocks, rows, blocks,
            blocks, blocks, rows, rows, blocks, blocks,
        ),
        out_specs=(
            rows, whole, whole, whole, rows, rows, rows, blocks, rows, blocks,
            blocks, blocks, rows, rows, blocks, blocks,
        ),
        check_vma=False,
    )
```

time: 156 us -> 78 us (0.50)
  blocking collectives: 63.1 us -> 0 us
  Pallas kernels: 0 us -> 10.7 us
  local copies, waits for them, and re-layouts: 14.4 us -> 4.72 us
  matrix products: 21.8 us -> 13 us
  starting transfers between devices: 20.9 us -> 15.9 us
  other arithmetic: 5.04 us -> 2.09 us
  waiting for transfers between devices: 29 us -> 30.6 us
    psum x1 -> x0, blocking collectives: 63.1 us -> none  [per_device(): centre_total = lax.psum(centre_part, ('group', 'member'))]
    pallas_call x0 -> x3, Pallas kernels: none -> 10.7 us  [the longest x1 6.82 us: per_device(): pl.pallas_call(expert_kernel, out_shape=(jax.ShapeDtypeStruct((devices, s...]
    dot_general x9 -> x2, matrix products: 21.8 us -> 13 us  [the longest x1 8.19 us: per_device(): lax.dot_general(latents, backward, TN, preferred_element_type=jnp.float32)]
    all_to_all x3 -> x2, starting transfers between devices: 20.9 us -> 15.9 us  [the longest x1 11.1 us: per_device(): lax.all_to_all(packed, AXES, split_axis=0, concat_axis=0, tiled=True)]
    scatter x2 -> x0, local copies, waits for them, and re-layouts: 4.76 us -> none  [the longest x1 2.6 us: per_device(): jnp.zeros((devices * slot_cap, feature_count), jnp.bfloat16).at[position]]
    unnamed x42 -> x38, local copies, waits for them, and re-layouts: 0.14 us -> 4.71 us
    reshape x4 -> x1, local copies, waits for them, and re-layouts: 2.9 us -> 0.01 us  [per_device(): centre_total = jnp.sum(returned[:, :slot_cap - 1, features:].astype(jnp.f...]
    gather x1 -> x0, local copies, waits for them, and re-layouts: 2.2 us -> none  [per_device(): recon = returned.reshape(devices * slot_cap, feature_count)[position]]
  transfers between devices with their start and end apart: 3 -> 2, of which waited for: 3 -> 2; matrix products, arithmetic and copies ran while one was open for 13% -> 18% of each run, Pallas kernels for 0% -> 0%
where the time goes in v1:
time: 78 us; the launch traced here: 77.7 us
  waiting for transfers between devices  30.6 us (39%)
  starting transfers between devices  15.9 us (20%)
  matrix products  13 us (17%)
  Pallas kernels  10.7 us (14%)
  local copies, waits for them, and re-layouts  4.72 us (6%)
  other arithmetic  2.09 us (3%)
    all_to_all x1, waiting for transfers between devices, per_device(): lax.all_to_all(packed, AXES, split_axis=0, concat_axis=0, tiled=True)  20.4 us
    all_to_all x1, starting transfers between devices, per_device(): lax.all_to_all(packed, AXES, split_axis=0, concat_axis=0, tiled=True)  11.1 us
    all_to_all x1, waiting for transfers between devices, per_device(): lax.all_to_all(outgoing, AXES, split_axis=0, concat_axis=0, tiled=True)  10.2 us
    dot_general x1, matrix products, per_device(): lax.dot_general(latents, backward, TN, preferred_element_type=jnp.float32)  8.19 us
    pallas_call x1, Pallas kernels, per_device(): pl.pallas_call(expert_kernel, out_shape=(jax.ShapeDtypeStruct((devices, s...  6.82 us
    all_to_all x1, starting transfers between devices, per_device(): lax.all_to_all(outgoing, AXES, split_axis=0, concat_axis=0, tiled=True)  4.79 us
    dot_general x1, matrix products, per_device(): lax.dot_general(centred, preact_grad, TN, preferred_element_type=jnp.floa...  4.77 us
    unnamed x38, local copies, waits for them, and re-layouts  4.71 us
  transfers between devices with their start and end apart: 2, of which 2 were waited for; matrix products, arithmetic and copies ran while one was open for 18% of the time, Pallas kernels for 0%

profile of v1, /device:TPU:0, one launch (start us, length us, event | category | flops | bytes accessed | tf_op | source)
XLA Modules:
  0.0 77.7 jit_solution(11455753051817268805)
XLA Ops:
  0.6 0.0 copy-start
  0.7 0.0 copy-start.1
  0.7 1.1 %copy-done.1 = bf16[256,1152]{1,0:T(8,128)(2,1)S(1)} copy-done((bf16[256,1152]{1,0:T(8,128)(2,1)S(1)}, bf16[256,1152]{1,0:T(8,128)(2,1)}, u32[]{:S(2)}) %copy-start.1) | copy-done | bytes 589848
  1.8 0.0 copy-start.4
  1.8 0.7 copy-done.4
  2.5 0.0 copy-start.10
  2.5 0.0 copy-start.2
  2.5 0.0 copy-start.3
  2.5 2.0 %pack.1 = bf16[128,4,1152]{2,1,0:T(4,128)(2,1)} custom-call(s32[1,256]{1,0:T(1,128)S(1)} %bitcast.46, bf16[256,1152]{1,0:T(8,128)(2,1)S(1)} %copy-done.1), custom_call_target="tpu_custom_call" | custom-call | tf_op jit(solution)/shard_map/pack/pallas_call | solution.py:197
  4.5 11.1 %all-to-all-start = ((bf16[128,4,1152]{2,1,0:T(4,128)(2,1)}), bf16[128,4,1152]{2,1,0:T(4,128)(2,1)S(1)}, u32[]{:S(2)}, u32[]{:S(2)}) async-start(bf16[128,4,1152]{2,1,0:T(4,128)(2,1)} %pack.1), calls=%async_computation | async-start | bytes 2359296 | tf_op jit(solution)/shard_map/all_to_all | solution.py:203
  15.6 0.0 copy-done.10
  15.7 20.4 %all-to-all-done.arrived_ref = bf16[128,4,1152]{2,1,0:T(4,128)(2,1)S(1)} async-done(((bf16[128,4,1152]{2,1,0:T(4,128)(2,1)}), bf16[128,4,1152]{2,1,0:T(4,128)(2,1)S(1)}, u32[]{:S(2)}, u32[]{:S(2)}) %all-to-all-start) | async-done | bytes 1179680 | tf_op jit(solution)/shard_map/all_to_all | solution.py:203
  36.1 0.0 copy-done
  36.1 0.0 copy-done.2
  36.1 0.0 copy-done.3
  36.1 6.8 %expert.1 = (bf16[128,4,1536]{2,1,0:T(4,128)(2,1)}, bf16[512,1152]{1,0:T(8,128)(2,1)S(1)}, bf16[512,512]{1,0:T(8,128)(2,1)S(1)}, bf16[512,1152]{1,0:T(8,128)(2,1...) custom-call(bf16[128,4,1152]{2,1,0:T(4,128)(2,1)S(1)} %all-to-all-done.arrived_ref, ...), custom_call_target="tpu_custom_call" | custom-call | tf_op jit(solution)/shard_map/expert/pallas_call | solution.py:204
  42.9 0.0 copy-start.6
  42.9 1.0 %copy-done.6 = bf16[512,1152]{1,0:T(8,128)(2,1)} copy-done((bf16[512,1152]{1,0:T(8,128)(2,1)}, bf16[512,1152]{1,0:T(8,128)(2,1)S(1)}, u32[]{:S(2)}) %copy-start.6) | copy-done | bytes 1179672
  43.9 0.0 copy-start.8
  43.9 1.0 %copy-done.8 = bf16[512,1152]{1,0:T(8,128)(2,1)} copy-done((bf16[512,1152]{1,0:T(8,128)(2,1)}, bf16[512,1152]{1,0:T(8,128)(2,1)S(1)}, u32[]{:S(2)}) %copy-start.8) | copy-done | bytes 1179672
  44.9 0.0 copy-start.9
  44.9 0.8 %copy-done.9 = bf16[512,512]{1,0:T(8,128)(2,1)} copy-done((bf16[512,512]{1,0:T(8,128)(2,1)}, bf16[512,512]{1,0:T(8,128)(2,1)S(1)}, u32[]{:S(2)}) %copy-start.9) | copy-done | bytes 524312
  45.7 0.0 copy-start.13
  45.7 0.0 copy-start.14
  45.7 0.0 copy-start.15
  45.7 0.0 copy-start.16
  45.7 4.8 %all-to-all-start.1 = ((bf16[128,4,1536]{2,1,0:T(4,128)(2,1)}), bf16[128,4,1536]{2,1,0:T(4,128)(2,1)S(1)}, u32[]{:S(2)}, u32[]{:S(2)}) async-start(bf16[128,4,1536]{2,1,0:T(4,128)(2,1)} %get-tuple-element.23), calls=%async_computation.1 | async-start | bytes 3145728 | tf_op jit(solution)/shard_map/all_to_all | solution.py:222
  50.5 0.0 copy-done.13
  50.5 0.0 copy-done.14
  50.5 0.6 subtract_convert_fusion.2
  51.2 0.0 copy-done.15
  51.2 0.0 copy-done.16
  51.2 0.6 divide_subtract_fusion.1
  51.8 0.0 copy-start.7
  51.8 0.0 copy-start.17
  51.8 0.0 copy-start.18
  51.8 8.2 %fusion.6 = (f32[1,512,1152]{2,1,0:T(8,128)}, bf16[1,512,1152]{2,1,0:T(8,128)(2,1)}, f32[1,512,1152]{2,1,0:T(8,128)}) fusion(f32[1,512,1152]{2,1,0:T(8,128)} %param.33, f32[1,512,1152]{2,1,0:T(8,128)} %param.32, bf16[1,512,1152]{2,1,0:T(8,128)(2,1)} %param.27, bf16[512,512]{1,0:T(8,128)(2,1)} %copy-done.9, bf16[512,1152]{1,0:T(8,128)(2,1)} %copy-done.8), kind=kOutput, calls=%fused_computation.13 | convolution fusion | flops 612237312 | bytes 13500416 | tf_op jit(solution)/shard_map/dot_general | solution.py:223
  60.0 0.0 copy-done.7
  60.0 0.0 copy-done.17
  60.0 0.0 copy-done.18
  60.0 0.0 copy-start.11
  60.0 0.0 copy-start.12
  60.0 0.0 copy-start.5
  60.0 4.8 %fusion.7 = (f32[1,1152,512]{2,1,0:T(8,128)}, bf16[1,1152,512]{2,1,0:T(8,128)(2,1)}, f32[1,1152,512]{2,1,0:T(8,128)}) fusion(f32[1,1152,512]{2,1,0:T(8,128)S(1)} %copy-done.17, f32[1,1152,512]{2,1,0:T(8,128)S(1)} %copy-done.18, bf16[1,1152,512]{2,1,0:T(8,128)(2,1)S(1)} %copy-done, bf16[512,1152]{1,0:T(8,128)(2,1)S(1)} %copy-done.7, ...), kind=kOutput, calls=%fused_computation.14 | convolution fusion | flops 612237312 | bytes 13500416 | tf_op jit(solution)/shard_map/dot_general | solution.py:224
  64.8 10.2 %all-to-all-done.1.returned_ref = bf16[128,4,1536]{2,1,0:T(4,128)(2,1)S(1)} async-done(((bf16[128,4,1536]{2,1,0:T(4,128)(2,1)}), bf16[128,4,1536]{2,1,0:T(4,128)(2,1)S(1)}, u32[]{:S(2)}, u32[]{:S(2)}) %all-to-all-start.1) | async-done | bytes 1572896 | tf_op jit(solution)/shard_map/all_to_all | solution.py:222
  75.0 0.2 convert_reduce_fusion
  75.2 0.0 copy-done.11
  75.2 0.0 copy-done.12
  75.2 0.6 divide_subtract_fusion
  75.8 0.0 copy-done.5
  75.9 1.9 %unpack.1 = bf16[256,1152]{1,0:T(8,128)(2,1)} custom-call(s32[1,256]{1,0:T(1,128)S(1)} %bitcast.47, bf16[128,4,1536]{2,1,0:T(4,128)(2,1)S(1)} %all-to-all-done.1.returned_ref), custom_call_target="tpu_custom_call" | custom-call | tf_op jit(solution)/shard_map/unpack/pallas_call | solution.py:229
  (2 shorter events, 0.0 us)
Async XLA Ops:
  0.6 35.4 %copy-start = (bf16[1,1152,512]{2,1,0:T(8,128)(2,1)S(1)}, bf16[1,1152,512]{2,1,0:T(8,128)(2,1)}, u32[]{:S(2)}) copy-start(bf16[1,1152,512]{2,1,0:T(8,128)(2,1)} %param.25) | copy-start | bytes 3538948
  0.7 1.2 %copy-start.1 = (bf16[256,1152]{1,0:T(8,128)(2,1)S(1)}, bf16[256,1152]{1,0:T(8,128)(2,1)}, u32[]{:S(2)}) copy-start(bf16[256,1152]{1,0:T(8,128)(2,1)} %rows_ref.1) | copy-start | bytes 1769476
  1.8 0.7 copy-start.4
  2.5 13.2 %copy-start.10 = (f32[1152]{0:T(1024)S(1)}, f32[1152]{0:T(1024)}, u32[]{:S(2)}) copy-start(f32[1152]{0:T(1024)} %param.19) | copy-start | bytes 13828
  2.5 33.6 %copy-start.2 = (bf16[1,1152]{1,0:T(2,128)(2,1)S(1)}, bf16[1,1152]{1,0:T(2,128)(2,1)}, u32[]{:S(2)}) copy-start(bf16[1,1152]{1,0:T(2,128)(2,1)} %router_ref.1) | copy-start | bytes 6916
  2.5 33.6 %copy-start.3 = (f32[1,512]{1,0:T(1,128)S(1)}, f32[1,512]{1,0:T(1,128)}, u32[]{:S(2)}) copy-start(f32[1,512]{1,0:T(1,128)} %bias_ref.1) | copy-start | bytes 6148
  4.5 31.6 %all-to-all-start = ((bf16[128,4,1152]{2,1,0:T(4,128)(2,1)}), bf16[128,4,1152]{2,1,0:T(4,128)(2,1)S(1)}, u32[]{:S(2)}, u32[]{:S(2)}) async-start(bf16[128,4,1152]{2,1,0:T(4,128)(2,1)} %pack.1), calls=%async_computation | async-start | bytes 2359296 | tf_op jit(solution)/shard_map/all_to_all | solution.py:203
  42.9 1.0 %copy-start.6 = (bf16[512,1152]{1,0:T(8,128)(2,1)}, bf16[512,1152]{1,0:T(8,128)(2,1)S(1)}, u32[]{:S(2)}) copy-start(bf16[512,1152]{1,0:T(8,128)(2,1)S(1)} %get-tuple-element.25) | copy-start | bytes 3538948
  43.9 1.0 %copy-start.8 = (bf16[512,1152]{1,0:T(8,128)(2,1)}, bf16[512,1152]{1,0:T(8,128)(2,1)S(1)}, u32[]{:S(2)}) copy-start(bf16[512,1152]{1,0:T(8,128)(2,1)S(1)} %get-tuple-element.29) | copy-start | bytes 3538948
  44.9 0.8 %copy-start.9 = (bf16[512,512]{1,0:T(8,128)(2,1)}, bf16[512,512]{1,0:T(8,128)(2,1)S(1)}, u32[]{:S(2)}) copy-start(bf16[512,512]{1,0:T(8,128)(2,1)S(1)} %get-tuple-element.28) | copy-start | bytes 1572868
  45.7 4.8 %copy-start.13 = (f32[1,1152]{1,0:T(1,128)S(1)}, f32[1,1152]{1,0:T(1,128)}, u32[]{:S(2)}) copy-start(f32[1,1152]{1,0:T(1,128)} %param.23) | copy-start | bytes 13828
  45.7 4.8 %copy-start.14 = (f32[1,1152]{1,0:T(1,128)S(1)}, f32[1,1152]{1,0:T(1,128)}, u32[]{:S(2)}) copy-start(f32[1,1152]{1,0:T(1,128)} %param.24) | copy-start | bytes 13828
  45.7 5.5 %copy-start.15 = (f32[1,512]{1,0:T(1,128)S(1)}, f32[1,512]{1,0:T(1,128)}, u32[]{:S(2)}) copy-start(f32[1,512]{1,0:T(1,128)} %param.30) | copy-start | bytes 6148
  45.7 5.5 %copy-start.16 = (f32[1,512]{1,0:T(1,128)S(1)}, f32[1,512]{1,0:T(1,128)}, u32[]{:S(2)}) copy-start(f32[1,512]{1,0:T(1,128)} %param.31) | copy-start | bytes 6148
  45.7 29.3 %all-to-all-start.1 = ((bf16[128,4,1536]{2,1,0:T(4,128)(2,1)}), bf16[128,4,1536]{2,1,0:T(4,128)(2,1)S(1)}, u32[]{:S(2)}, u32[]{:S(2)}) async-start(bf16[128,4,1536]{2,1,0:T(4,128)(2,1)} %get-tuple-element.23), calls=%async_computation.1 | async-start | bytes 3145728 | tf_op jit(solution)/shard_map/all_to_all | solution.py:222
  51.8 8.2 %copy-start.7 = (bf16[512,1152]{1,0:T(8,128)(2,1)S(1)}, bf16[512,1152]{1,0:T(8,128)(2,1)}, u32[]{:S(2)}) copy-start(bf16[512,1152]{1,0:T(8,128)(2,1)} %copy-done.6) | copy-start | bytes 3538948
  51.8 8.2 %copy-start.17 = (f32[1,1152,512]{2,1,0:T(8,128)S(1)}, f32[1,1152,512]{2,1,0:T(8,128)}, u32[]{:S(2)}) copy-start(f32[1,1152,512]{2,1,0:T(8,128)} %param.29) | copy-start | bytes 7077892
  51.8 8.2 %copy-start.18 = (f32[1,1152,512]{2,1,0:T(8,128)S(1)}, f32[1,1152,512]{2,1,0:T(8,128)}, u32[]{:S(2)}) copy-start(f32[1,1152,512]{2,1,0:T(8,128)} %param.28) | copy-start | bytes 7077892
  60.0 15.2 %copy-start.11 = (f32[1152]{0:T(1024)S(1)}, f32[1152]{0:T(1024)}, u32[]{:S(2)}) copy-start(f32[1152]{0:T(1024)} %param.20) | copy-start | bytes 13828
  60.0 15.2 %copy-start.12 = (f32[1152]{0:T(1024)S(1)}, f32[1152]{0:T(1024)}, u32[]{:S(2)}) copy-start(f32[1152]{0:T(1024)} %param.21) | copy-start | bytes 13828
  60.0 15.8 %copy-start.5 = (s32[256,1]{0,1:T(1,128)S(1)}, s32[256,1]{0,1:T(1,128)}, u32[]{:S(2)}) copy-start(s32[256,1]{0,1:T(1,128)} %param.18) | copy-start | bytes 3076

commit v2 on v1

v2 whole, which is shorter than its diff:
```python
import jax
import jax.numpy as jnp
from jax import lax
from jax.experimental import pallas as pl
from jax.experimental.pallas import tpu as pltpu
from jax.sharding import PartitionSpec as P

STEP = 10


learn_rate = 0.001
beta_one = 0.9
beta_two = 0.999
adam_eps = 1e-08
sparsity = 0.1

AXES = ("group", "member")
EMPTY_MARK = 64.0
EMPTY_LIMIT = 32.0
VMEM_LIMIT = 20 * 1024 * 1024
STEP_LIMIT = 36 * 1024 * 1024
NT = (((1,), (1,)), ((), ()))
TN = (((0,), (0,)), ((), ()))


def adam_update(weights_in, gradient, moment_one, moment_two):
    first_new = beta_one * moment_one + (1.0 - beta_one) * gradient
    second_new = beta_two * moment_two + (1.0 - beta_two) * gradient * gradient
    first_hat = first_new * (1.0 / (1.0 - beta_one**STEP))
    second_hat = second_new * (1.0 / (1.0 - beta_two**STEP))
    stepped = weights_in.astype(jnp.float32) - learn_rate * first_hat / (
        jnp.sqrt(second_hat) + adam_eps
    )
    return (stepped.astype(weights_in.dtype), first_new, second_new)


def slot_matrix(route_row, experts, slot_cap):
    rows = route_row.shape[1]
    onehot = lax.broadcasted_iota(jnp.int32, (experts, rows), 0) == route_row
    onehot = onehot.astype(jnp.float32)
    later = lax.broadcasted_iota(jnp.int32, (rows, rows), 0) < lax.broadcasted_iota(
        jnp.int32, (rows, rows), 1
    )
    before = jnp.dot(
        onehot.astype(jnp.bfloat16),
        later.astype(jnp.float32).astype(jnp.bfloat16),
        preferred_element_type=jnp.float32,
    )
    rank = jnp.sum(before * onehot, axis=0, keepdims=True).astype(jnp.int32)
    position = route_row * slot_cap + rank
    chosen = lax.broadcasted_iota(jnp.int32, (experts * slot_cap, rows), 0) == position
    return chosen.astype(jnp.float32)


def taken_kernel(route_ref, taken_ref):
    rows, slots = taken_ref.shape
    experts = lax.axis_size("group") * lax.axis_size("member")
    taken_ref[...] = slot_matrix(route_ref[...], experts, slots // experts).T.astype(jnp.bfloat16)


def pack_kernel(route_ref, rows_ref, packed_ref, route_vmem, rows_vmem, packed_vmem, sems):
    experts, slot_cap, features = packed_ref.shape
    fetch_route = pltpu.make_async_copy(route_ref, route_vmem, sems.at[1])
    fetch_route.start()
    fetch = pltpu.make_async_copy(rows_ref, rows_vmem, sems.at[0])
    fetch.start()
    fetch_route.wait()
    chosen = slot_matrix(route_vmem[...], experts, slot_cap)
    mark = (1.0 - jnp.sum(chosen, axis=1, keepdims=True)) * EMPTY_MARK
    chosen = chosen.astype(jnp.bfloat16)
    fetch.wait()
    copies = []
    for i, (start, width) in enumerate(column_blocks(features)):
        block = slice(start, start + width)
        part = jnp.dot(chosen, rows_vmem[:, block], preferred_element_type=jnp.float32)
        if start == 0:
            part = part + mark
        packed_vmem[:, :, block] = part.astype(jnp.bfloat16).reshape(experts, slot_cap, width)
        copies.append(
            pltpu.make_async_copy(
                packed_vmem.at[:, :, block], packed_ref.at[:, :, block], sems.at[1 + i]
            )
        )
        copies[-1].start()
    for copy in copies:
        copy.wait()


def unpack_kernel(
    taken_ref, returned_ref, centre_ref, first_ref, second_ref,
    recon_ref, new_centre_ref, new_first_ref, new_second_ref,
):
    experts, slot_cap, wide = returned_ref.shape
    features = recon_ref.shape[1]
    tail = wide - features
    taken = taken_ref[...]
    for start, width in column_blocks(features):
        block = slice(start, start + width)
        returned = returned_ref[:, :, block].reshape(experts * slot_cap, width)
        recon_ref[:, block] = jnp.dot(
            taken, returned, preferred_element_type=jnp.float32
        ).astype(jnp.bfloat16)
    total = jnp.sum(returned_ref[:, :, features:].astype(jnp.float32), axis=0)
    for i in range(features // tail):
        block = slice(i * tail, (i + 1) * tail)
        updated = adam_update(
            centre_ref[:, block], total[i : i + 1], first_ref[:, block], second_ref[:, block]
        )
        for value, target in zip(updated, (new_centre_ref, new_first_ref, new_second_ref)):
            target[block] = value.reshape(tail)


def column_blocks(features, width=256):
    return [(start, min(width, features - start)) for start in range(0, features, width)]


def expert_kernel(
    arrived_ref,
    centre_ref,
    router_ref,
    encoder_ref,
    bias_ref,
    decoder_hbm,
    outgoing_hbm,
    rows_hbm,
    latents_hbm,
    backward_hbm,
    preact_grad_hbm,
    bias_grad_ref,
    logit_grad_ref,
    rows_ref,
    latents_ref,
    backward_ref,
    preact_grad_ref,
    centred_ref,
    decoder_ref,
    outgoing_ref,
    positive_ref,
    sems,
    side_sems,
):
    sources, slot_cap, features = arrived_ref.shape
    count = sources * slot_cap
    tail = outgoing_ref.shape[2] - features
    fetch = pltpu.make_async_copy(decoder_hbm, decoder_ref, sems.at[0])
    fetch.start()
    copies = []

    def write_out(source, target, sem):
        copies.append(pltpu.make_async_copy(source, target, sem))
        copies[-1].start()

    centre = centre_ref[...]
    live = None
    for start, width in column_blocks(features):
        block = slice(start, start + width)
        wide_rows = arrived_ref[:, :, block].reshape(count, width)
        if live is None:
            live = wide_rows[:, 0:1].astype(jnp.float32) < EMPTY_LIMIT
            wide_rows = jnp.where(live, wide_rows.astype(jnp.float32), 0.0).astype(jnp.bfloat16)
        rows_ref[:, block] = wide_rows
        centred_ref[:, block] = (wide_rows.astype(jnp.float32) - centre[:, block]).astype(
            jnp.bfloat16
        )
    write_out(rows_ref, rows_hbm, side_sems.at[0])
    live_mask = live.astype(jnp.float32)
    logits = lax.dot_general(
        rows_ref[...],
        jnp.broadcast_to(router_ref[...], (8, features)),
        NT,
        preferred_element_type=jnp.float32,
    )[:, 0:1]
    gating = jax.nn.sigmoid(logits)
    for start, width in column_blocks(encoder_ref.shape[1]):
        block = slice(start, start + width)
        preact = (
            jnp.dot(centred_ref[...], encoder_ref[:, block], preferred_element_type=jnp.float32)
            + bias_ref[:, block]
        )
        positive = jnp.maximum(preact, 0.0)
        positive_ref[:, block] = positive * live_mask
        latents_ref[:, block] = (positive * positive).astype(jnp.bfloat16)
    write_out(latents_ref, latents_hbm, side_sems.at[1])
    fetch.wait()
    projected = jnp.zeros((count, 1), jnp.float32)
    error_sums = []
    for i, (start, width) in enumerate(column_blocks(features)):
        block = slice(start, start + width)
        ungated = jnp.dot(
            latents_ref[...], decoder_ref[:, block], preferred_element_type=jnp.float32
        )
        rebuilt = centre[:, block] + gating * ungated
        outgoing_ref[:, :, block] = rebuilt.astype(jnp.bfloat16).reshape(sources, slot_cap, width)
        write_out(outgoing_ref.at[:, :, block], outgoing_hbm.at[:, :, block], sems.at[1 + i])
        errors = (rows_ref[:, block].astype(jnp.float32) - rebuilt) * live_mask
        backward_ref[:, block] = (-gating * errors).astype(jnp.bfloat16)
        projected = projected + jnp.sum(errors * ungated, axis=1, keepdims=True)
        error_sums.append(jnp.sum(errors, axis=0, keepdims=True))
    write_out(backward_ref, backward_hbm, side_sems.at[2])
    logit_grad_ref[...] = -projected * gating * (1.0 - gating)
    bias_grads = []
    for start, width in column_blocks(encoder_ref.shape[1]):
        block = slice(start, start + width)
        latent_grad = lax.dot_general(
            backward_ref[...], decoder_ref[block, :], NT, preferred_element_type=jnp.float32
        )
        preact_grad = ((latent_grad + sparsity) * 2.0 * positive_ref[:, block]).astype(jnp.bfloat16)
        preact_grad_ref[:, block] = preact_grad
        bias_grads.append(jnp.sum(preact_grad.astype(jnp.float32), axis=0, keepdims=True))
    write_out(preact_grad_ref, preact_grad_hbm, side_sems.at[3])
    bias_grad = jnp.concatenate(bias_grads, axis=1)
    bias_grad_ref[...] = bias_grad
    high = bias_grad.astype(jnp.bfloat16).astype(jnp.float32)
    middle = (bias_grad - high).astype(jnp.bfloat16).astype(jnp.float32)
    low = bias_grad - high - middle
    row = lax.broadcasted_iota(jnp.int32, (8, 1), 0)
    terms = jnp.where(row == 0, high, jnp.where(row == 1, middle, jnp.where(row == 2, low, 0.0)))
    passed = jnp.sum(
        lax.dot_general(
            terms.astype(jnp.bfloat16), encoder_ref[...], NT, preferred_element_type=jnp.float32
        ),
        axis=0,
        keepdims=True,
    )
    centre_part = -jnp.concatenate(error_sums, axis=1) - passed
    pieces = [centre_part[:, i * tail : (i + 1) * tail] for i in range(features // tail)]
    pieces += [jnp.zeros((1, tail), jnp.float32)] * (slot_cap - len(pieces))
    outgoing_ref[:, :, features:] = jnp.broadcast_to(
        jnp.concatenate(pieces, axis=0).astype(jnp.bfloat16)[None], (sources, slot_cap, tail)
    )
    write_out(outgoing_ref.at[:, :, features:], outgoing_hbm.at[:, :, features:], sems.at[0])
    for copy in copies:
        copy.wait()


def step_kernel(centre_ref, *refs):
    sources, targets = refs[:10], refs[10:16]
    arrived, made, (in_sems, out_sems) = refs[16:26], refs[26:32], refs[32:]
    rows, preact_grad, latents, backward = arrived[:4]
    plan = (
        (rows, preact_grad, (0, 1), (4, 5, 6), (0, 1, 2)),
        (latents, backward, (2, 3), (7, 8, 9), (3, 4, 5)),
    )
    fetches, started = [], 0
    for left, right, whole, state, _ in plan:
        waits = []
        for i in whole:
            waits.append(pltpu.make_async_copy(sources[i], arrived[i], in_sems.at[started]))
            started += 1
        for start, width in column_blocks(left.shape[1]):
            block = slice(start, start + width)
            for i in state:
                waits.append(
                    pltpu.make_async_copy(
                        sources[i].at[block, :], arrived[i].at[block, :], in_sems.at[started]
                    )
                )
                started += 1
            fetches.append(waits)
            waits = []
    for waits in fetches:
        for copy in waits:
            copy.start()
    copies = []
    fetched = iter(fetches)
    for left, right, _, state, made_here in plan:
        weights, first, second = (arrived[i] for i in state)
        for start, width in column_blocks(left.shape[1]):
            block = slice(start, start + width)
            for copy in next(fetched):
                copy.wait()
            turned = left[:, block]
            if left is rows:
                turned = (turned.astype(jnp.float32) - centre_ref[:, block]).astype(jnp.bfloat16)
            gradient = lax.dot_general(turned, right[...], TN, preferred_element_type=jnp.float32)
            updated = adam_update(weights[block, :], gradient, first[block, :], second[block, :])
            for value, i in zip(updated, made_here):
                made[i][block, :] = value
                copies.append(
                    pltpu.make_async_copy(
                        made[i].at[block, :], targets[i].at[block, :], out_sems.at[len(copies)]
                    )
                )
                copies[-1].start()
    for copy in copies:
        copy.wait()


def in_hbm(*arrays):
    return [pltpu.with_memory_space_constraint(array, pltpu.HBM) for array in arrays]


def per_device(
    activations,
    routes,
    centre_bias,
    centre_first,
    centre_second,
    router,
    router_first,
    router_second,
    encoder,
    enc_bias,
    decoder,
    encoder_first,
    encoder_second,
    enc_bias_first,
    enc_bias_second,
    decoder_first,
    decoder_second,
):
    devices = lax.axis_size("group") * lax.axis_size("member")
    row_count, features = activations.shape
    latent_count = encoder.shape[2]
    slot_cap = 2 * row_count // devices
    count = devices * slot_cap
    wide = features + features // (slot_cap - 1)
    params = pltpu.CompilerParams(vmem_limit_bytes=VMEM_LIMIT)
    hbm = pl.BlockSpec(memory_space=pltpu.HBM)
    local = pl.BlockSpec(memory_space=pltpu.VMEM)
    copies = len(column_blocks(features)) + 1
    route_row = routes.reshape(1, row_count)
    packed = pl.pallas_call(
        pack_kernel,
        in_specs=[hbm, hbm],
        out_specs=hbm,
        out_shape=pltpu.HBM((devices, slot_cap, features), jnp.bfloat16),
        scratch_shapes=[
            pltpu.VMEM((1, row_count), jnp.int32),
            pltpu.VMEM((row_count, features), jnp.bfloat16),
            pltpu.VMEM((devices, slot_cap, features), jnp.bfloat16),
            pltpu.SemaphoreType.DMA((copies,)),
        ],
        compiler_params=pltpu.CompilerParams(vmem_limit_bytes=VMEM_LIMIT),
        name="pack",
    )(*in_hbm(route_row, activations))
    arrived = lax.all_to_all(packed, AXES, split_axis=0, concat_axis=0, tiled=True)
    (outgoing, rows, latents, backward, preact_grad, bias_grad, logit_grad) = pl.pallas_call(
        expert_kernel,
        in_specs=[local, local, local, local, local, hbm],
        out_specs=(hbm,) * 5 + (local,) * 2,
        out_shape=(
            pltpu.HBM((devices, slot_cap, wide), jnp.bfloat16),
            pltpu.HBM((count, features), jnp.bfloat16),
            pltpu.HBM((count, latent_count), jnp.bfloat16),
            pltpu.HBM((count, features), jnp.bfloat16),
            pltpu.HBM((count, latent_count), jnp.bfloat16),
            jax.ShapeDtypeStruct((1, latent_count), jnp.float32),
            jax.ShapeDtypeStruct((count, 1), jnp.float32),
        ),
        scratch_shapes=[
            pltpu.VMEM((count, features), jnp.bfloat16),
            pltpu.VMEM((count, latent_count), jnp.bfloat16),
            pltpu.VMEM((count, features), jnp.bfloat16),
            pltpu.VMEM((count, latent_count), jnp.bfloat16),
            pltpu.VMEM((count, features), jnp.bfloat16),
            pltpu.VMEM((latent_count, features), jnp.bfloat16),
            pltpu.VMEM((devices, slot_cap, wide), jnp.bfloat16),
            pltpu.VMEM((count, latent_count), jnp.float32),
            pltpu.SemaphoreType.DMA((copies,)),
            pltpu.SemaphoreType.DMA((4,)),
        ],
        compiler_params=pltpu.CompilerParams(vmem_limit_bytes=VMEM_LIMIT),
        name="expert",
    )(
        arrived,
        centre_bias[None],
        router,
        encoder[0],
        enc_bias,
        *in_hbm(decoder[0]),
    )
    returned = lax.all_to_all(outgoing, AXES, split_axis=0, concat_axis=0, tiled=True)
    router_grad = jnp.dot(
        logit_grad.astype(jnp.bfloat16).T, rows, preferred_element_type=jnp.float32
    )
    router_new = adam_update(router, router_grad, router_first, router_second)
    bias_new = adam_update(enc_bias, bias_grad, enc_bias_first, enc_bias_second)
    matrices = (
        encoder[0], encoder_first[0], encoder_second[0],
        decoder[0], decoder_first[0], decoder_second[0],
    )
    operands = (rows, preact_grad, latents, backward) + matrices
    pieces = 3 * (len(column_blocks(features)) + len(column_blocks(latent_count)))
    stepped = pl.pallas_call(
        step_kernel,
        in_specs=[local] + [hbm] * 10,
        out_specs=(hbm,) * 6,
        out_shape=tuple(pltpu.HBM(array.shape, array.dtype) for array in matrices),
        scratch_shapes=[pltpu.VMEM(array.shape, array.dtype) for array in operands + matrices]
        + [pltpu.SemaphoreType.DMA((pieces + 4,)), pltpu.SemaphoreType.DMA((pieces,))],
        compiler_params=pltpu.CompilerParams(vmem_limit_bytes=STEP_LIMIT),
        cost_estimate=pl.CostEstimate(
            flops=4 * count * features * latent_count,
            bytes_accessed=20 * features * latent_count,
            transcendentals=0,
        ),
        name="step",
    )(centre_bias[None], *in_hbm(*operands))
    encoder_new, decoder_new = stepped[:3], stepped[3:]
    taken = pl.pallas_call(
        taken_kernel,
        out_shape=jax.ShapeDtypeStruct((row_count, count), jnp.bfloat16),
        compiler_params=pltpu.CompilerParams(vmem_limit_bytes=VMEM_LIMIT),
        name="taken",
    )(route_row)
    recon, *centre_new = pl.pallas_call(
        unpack_kernel,
        out_shape=(jax.ShapeDtypeStruct((row_count, features), jnp.bfloat16),)
        + (jax.ShapeDtypeStruct((features,), jnp.float32),) * 3,
        compiler_params=params,
        name="unpack",
    )(taken, returned, centre_bias[None], centre_first[None], centre_second[None])
    return (
        recon,
        centre_new[0],
        centre_new[1],
        centre_new[2],
        router_new[0],
        router_new[1],
        router_new[2],
        encoder_new[0][None],
        bias_new[0],
        decoder_new[0][None],
        encoder_new[1][None],
        encoder_new[2][None],
        bias_new[1],
        bias_new[2],
        decoder_new[1][None],
        decoder_new[2][None],
    )


def solution(mesh):
    whole, rows, blocks = P(), P(AXES, None), P(AXES, None, None)
    return jax.shard_map(
        per_device,
        mesh=mesh,
        in_specs=(
            rows, rows, whole, whole, whole, rows, rows, rows, blocks, rows, blocks,
            blocks, blocks, rows, rows, blocks, blocks,
        ),
        out_specs=(
            rows, whole, whole, whole, rows, rows, rows, blocks, rows, blocks,
            blocks, blocks, rows, rows, blocks, blocks,
        ),
        check_vma=False,
    )
```

time: 78 us -> 70.6 us (0.905)
  matrix products: 13 us -> 0.27 us
  Pallas kernels: 10.7 us -> 20.3 us
  local copies, waits for them, and re-layouts: 4.72 us -> 0.47 us
    dot_general x2 -> x1, matrix products: 13 us -> 0.27 us  [per_device(): jnp.dot(logit_grad.astype(jnp.bfloat16).T, rows, preferred_element_type=j...]
    pallas_call x3 -> x5, Pallas kernels: 10.7 us -> 20.3 us  [the longest x1 11.2 us: per_device(): pl.pallas_call(step_kernel, in_specs=[local] + [hbm] * 10, out_specs=(hbm...]
    unnamed x38 -> x24, local copies, waits for them, and re-layouts: 4.71 us -> 0.45 us
  transfers between devices with their start and end apart: 2 -> 2, of which waited for: 2 -> 2; matrix products, arithmetic and copies ran while one was open for 18% -> 2% of each run, Pallas kernels for 0% -> 16%
where the time goes in v2:
time: 70.6 us; the launch traced here: 70.2 us
  waiting for transfers between devices  31.1 us (44%)
  Pallas kernels  20.3 us (29%)
  starting transfers between devices  15.8 us (22%)
  other arithmetic  1.38 us (2%)
  between operations  0.87 us (1%)
    all_to_all x1, waiting for transfers between devices, per_device(): lax.all_to_all(packed, AXES, split_axis=0, concat_axis=0, tiled=True)  20.4 us
    pallas_call x1, Pallas kernels, per_device(): pl.pallas_call(step_kernel, in_specs=[local] + [hbm] * 10, out_specs=(hbm...  11.2 us
    all_to_all x1, starting transfers between devices, per_device(): lax.all_to_all(packed, AXES, split_axis=0, concat_axis=0, tiled=True)  11.1 us
    all_to_all x1, waiting for transfers between devices, per_device(): lax.all_to_all(outgoing, AXES, split_axis=0, concat_axis=0, tiled=True)  10.8 us
    pallas_call x1, Pallas kernels, per_device(): pl.pallas_call(expert_kernel, in_specs=[local, local, local, local, local...  5.05 us
    all_to_all x1, starting transfers between devices, per_device(): lax.all_to_all(outgoing, AXES, split_axis=0, concat_axis=0, tiled=True)  4.66 us
    pallas_call x1, Pallas kernels, per_device(): pl.pallas_call(pack_kernel, in_specs=[hbm, hbm], out_specs=hbm, out_shape...  2.42 us
  transfers between devices with their start and end apart: 2, of which 2 were waited for; matrix products, arithmetic and copies ran while one was open for 2% of the time, Pallas kernels for 16%

profile of v2, /device:TPU:0, one launch (start us, length us, event | category | flops | bytes accessed | tf_op | source)
XLA Modules:
  0.0 70.2 jit_solution(15223786539805407242)
XLA Ops:
  0.6 2.4 %pack.1 = bf16[128,4,1152]{2,1,0:T(4,128)(2,1)} custom-call(s32[1,256]{1,0:T(1,128)} %bitcast.17, bf16[256,1152]{1,0:T(8,128)(2,1)} %rows_ref.1), custom_call_target="tpu_custom_call" | custom-call | tf_op jit(solution)/shard_map/pack/pallas_call | solution.py:323
  3.1 0.0 copy-start.5
  3.1 0.0 copy-start
  3.1 0.0 copy-start.1
  3.1 0.0 copy-start.2
  3.1 11.1 %all-to-all-start = ((bf16[128,4,1152]{2,1,0:T(4,128)(2,1)}), bf16[128,4,1152]{2,1,0:T(4,128)(2,1)S(1)}, u32[]{:S(2)}, u32[]{:S(2)}) async-start(bf16[128,4,1152]{2,1,0:T(4,128)(2,1)} %pack.1), calls=%async_computation | async-start | bytes 2359296 | tf_op jit(solution)/shard_map/all_to_all | solution.py:337
  14.3 0.0 copy-done.5
  14.3 20.4 %all-to-all-done.arrived_ref = bf16[128,4,1152]{2,1,0:T(4,128)(2,1)S(1)} async-done(((bf16[128,4,1152]{2,1,0:T(4,128)(2,1)}), bf16[128,4,1152]{2,1,0:T(4,128)(2,1)S(1)}, u32[]{:S(2)}, u32[]{:S(2)}) %all-to-all-start) | async-done | bytes 1179680 | tf_op jit(solution)/shard_map/all_to_all | solution.py:337
  34.7 0.0 copy-done
  34.7 0.0 copy-done.1
  34.7 0.0 copy-done.2
  34.7 5.1 %expert.1 = (bf16[128,4,1536]{2,1,0:T(4,128)(2,1)}, bf16[512,1152]{1,0:T(8,128)(2,1)}, bf16[512,512]{1,0:T(8,128)(2,1)}, bf16[512,1152]{1,0:T(8,128)(2,1)}, bf16...) custom-call(bf16[128,4,1152]{2,1,0:T(4,128)(2,1)S(1)} %all-to-all-done.arrived_ref, ...), custom_call_target="tpu_custom_call" | custom-call | tf_op jit(solution)/shard_map/expert/pallas_call | solution.py:338
  39.8 0.0 copy-start.3
  39.8 0.0 copy-start.6
  39.8 0.0 copy-start.7
  39.8 4.7 %all-to-all-start.1 = ((bf16[128,4,1536]{2,1,0:T(4,128)(2,1)}), bf16[128,4,1536]{2,1,0:T(4,128)(2,1)S(1)}, u32[]{:S(2)}, u32[]{:S(2)}) async-start(bf16[128,4,1536]{2,1,0:T(4,128)(2,1)} %get-tuple-element.33), calls=%async_computation.1 | async-start | bytes 3145728 | tf_op jit(solution)/shard_map/all_to_all | solution.py:373
  44.5 0.0 copy-done.3
  44.5 0.3 taken.1.taken_ref
  44.8 0.0 copy-done.6
  44.8 0.0 copy-done.7
  44.8 0.1 convert_reduce_fusion
  45.0 0.0 copy-start.4
  45.0 11.2 %step.1 = (bf16[1152,512]{1,0:T(8,128)(2,1)}, f32[1152,512]{1,0:T(8,128)}, f32[1152,512]{1,0:T(8,128)}, bf16[512,1152]{1,0:T(8,128)(2,1)}, f32[512,1152]{1,0:T(8,128)}, /*index=5*/f32[512,1152]{1,0:T(8,128)}) custom-call(f32[1,1152]{1,0:T(1,128)S(1)} %broadcast_in_dim.29.centre_ref, bf16[512,1152]{1,0:T(8,128)(2,1)} %get-tuple-element.39.refs_0_, ...), custom_call_target="tpu_custom_call" | custom-call | flops 1207959552 | bytes 11796480 | tf_op jit(solution)/shard_map/step/pallas_call | solution.py:385
  56.2 0.0 copy-done.4
  56.2 0.0 copy-start.10
  56.2 0.0 copy-start.11
  56.2 0.0 copy-start.8
  56.2 0.0 copy-start.9
  56.3 0.3 convolution_reduce_fusion
  56.5 0.4 copy-done.10
  56.9 0.0 copy-done.11
  56.9 0.6 divide_subtract_fusion
  57.5 0.0 copy-done.8
  57.5 0.0 copy-done.9
  57.5 0.6 subtract_convert_fusion
  58.2 10.8 %all-to-all-done.1.returned_ref = bf16[128,4,1536]{2,1,0:T(4,128)(2,1)S(1)} async-done(((bf16[128,4,1536]{2,1,0:T(4,128)(2,1)}), bf16[128,4,1536]{2,1,0:T(4,128)(2,1)S(1)}, u32[]{:S(2)}, u32[]{:S(2)}) %all-to-all-start.1) | async-done | bytes 1572896 | tf_op jit(solution)/shard_map/all_to_all | solution.py:373
  68.9 1.3 %unpack.1 = (bf16[256,1152]{1,0:T(8,128)(2,1)}, f32[1152]{0:T(1024)}, f32[1152]{0:T(1024)}, f32[1152]{0:T(1024)}) custom-call(bf16[256,512]{1,0:T(8,128)(2,1)S(1)} %taken.1.taken_ref, bf16[128,4,1536]{2,1,0:T(4,128)(2,1)S(1)} %all-to-all-done.1.returned_ref, f32[1,1152]{1,0:T(1,128)S(1)} %broadcast_in_dim.29.centre_ref, ...), custom_call_target="tpu_custom_call" | custom-call | tf_op jit(solution)/shard_map/unpack/pallas_call | solution.py:407
  (5 shorter events, 0.0 us)
Async XLA Ops:
  3.1 11.2 %copy-start.5 = (f32[1152]{0:T(1024)S(1)}, f32[1152]{0:T(1024)}, u32[]{:S(2)}) copy-start(f32[1152]{0:T(1024)} %param.19) | copy-start | bytes 13828
  3.1 31.6 %copy-start = (bf16[1,1152,512]{2,1,0:T(8,128)(2,1)S(1)}, bf16[1,1152,512]{2,1,0:T(8,128)(2,1)}, u32[]{:S(2)}) copy-start(bf16[1,1152,512]{2,1,0:T(8,128)(2,1)} %param.25) | copy-start | bytes 3538948
  3.1 31.6 %copy-start.1 = (bf16[1,1152]{1,0:T(2,128)(2,1)S(1)}, bf16[1,1152]{1,0:T(2,128)(2,1)}, u32[]{:S(2)}) copy-start(bf16[1,1152]{1,0:T(2,128)(2,1)} %router_ref.1) | copy-start | bytes 6916
  3.1 31.6 %copy-start.2 = (f32[1,512]{1,0:T(1,128)S(1)}, f32[1,512]{1,0:T(1,128)}, u32[]{:S(2)}) copy-start(f32[1,512]{1,0:T(1,128)} %bias_ref.1) | copy-start | bytes 6148
  3.1 31.6 %all-to-all-start = ((bf16[128,4,1152]{2,1,0:T(4,128)(2,1)}), bf16[128,4,1152]{2,1,0:T(4,128)(2,1)S(1)}, u32[]{:S(2)}, u32[]{:S(2)}) async-start(bf16[128,4,1152]{2,1,0:T(4,128)(2,1)} %pack.1), calls=%async_computation | async-start | bytes 2359296 | tf_op jit(solution)/shard_map/all_to_all | solution.py:337
  39.8 4.7 %copy-start.3 = (s32[256,1]{0,1:T(1,128)S(1)}, s32[256,1]{0,1:T(1,128)}, u32[]{:S(2)}) copy-start(s32[256,1]{0,1:T(1,128)} %param.18) | copy-start | bytes 3076
  39.8 5.0 %copy-start.6 = (f32[1152]{0:T(1024)S(1)}, f32[1152]{0:T(1024)}, u32[]{:S(2)}) copy-start(f32[1152]{0:T(1024)} %param.20) | copy-start | bytes 13828
  39.8 5.0 %copy-start.7 = (f32[1152]{0:T(1024)S(1)}, f32[1152]{0:T(1024)}, u32[]{:S(2)}) copy-start(f32[1152]{0:T(1024)} %param.21) | copy-start | bytes 13828
  39.8 29.1 %all-to-all-start.1 = ((bf16[128,4,1536]{2,1,0:T(4,128)(2,1)}), bf16[128,4,1536]{2,1,0:T(4,128)(2,1)S(1)}, u32[]{:S(2)}, u32[]{:S(2)}) async-start(bf16[128,4,1536]{2,1,0:T(4,128)(2,1)} %get-tuple-element.33), calls=%async_computation.1 | async-start | bytes 3145728 | tf_op jit(solution)/shard_map/all_to_all | solution.py:373
  45.0 11.2 %copy-start.4 = (bf16[512,1152]{1,0:T(8,128)(2,1)S(1)}, bf16[512,1152]{1,0:T(8,128)(2,1)}, u32[]{:S(2)}) copy-start(bf16[512,1152]{1,0:T(8,128)(2,1)} %get-tuple-element.39.refs_0_) | copy-start | bytes 3538948
  56.2 0.7 copy-start.10
  56.2 0.7 copy-start.11
  56.2 1.3 %copy-start.8 = (f32[1,1152]{1,0:T(1,128)S(1)}, f32[1,1152]{1,0:T(1,128)}, u32[]{:S(2)}) copy-start(f32[1,1152]{1,0:T(1,128)} %param.23) | copy-start | bytes 13828
  56.2 1.3 %copy-start.9 = (f32[1,1152]{1,0:T(1,128)S(1)}, f32[1,1152]{1,0:T(1,128)}, u32[]{:S(2)}) copy-start(f32[1,1152]{1,0:T(1,128)} %param.24) | copy-start | bytes 13828

commit v3 on v2

--- a/solution.py
+++ b/solution.py
@@ -19,6 +19,8 @@
 EMPTY_LIMIT = 32.0
 VMEM_LIMIT = 20 * 1024 * 1024
 STEP_LIMIT = 36 * 1024 * 1024
+PARTS = 1
+TAIL_COPIES = 4
 NT = (((1,), (1,)), ((), ()))
 TN = (((0,), (0,)), ((), ()))
 
@@ -151,64 +153,84 @@
         copies[-1].start()
 
     centre = centre_ref[...]
-    live = None
-    for start, width in column_blocks(features):
-        block = slice(start, start + width)
-        wide_rows = arrived_ref[:, :, block].reshape(count, width)
-        if live is None:
-            live = wide_rows[:, 0:1].astype(jnp.float32) < EMPTY_LIMIT
-            wide_rows = jnp.where(live, wide_rows.astype(jnp.float32), 0.0).astype(jnp.bfloat16)
-        rows_ref[:, block] = wide_rows
-        centred_ref[:, block] = (wide_rows.astype(jnp.float32) - centre[:, block]).astype(
-            jnp.bfloat16
-        )
+    router_rows = jnp.broadcast_to(router_ref[...], (8, features))
+    blocks = [slice(start, start + width) for start, width in column_blocks(features)]
+    latent_blocks = [
+        slice(start, start + width) for start, width in column_blocks(encoder_ref.shape[1])
+    ]
+    error_sums = [jnp.zeros((1, features), jnp.float32)]
+    bias_grads = [jnp.zeros((1, encoder_ref.shape[1]), jnp.float32)]
+    held = []
+    for part in range(PARTS):
+        rows = slice(part * count // PARTS, (part + 1) * count // PARTS)
+        owners = slice(part * sources // PARTS, (part + 1) * sources // PARTS)
+        live = None
+        for block in blocks:
+            wide_rows = arrived_ref[owners, :, block].reshape(
+                count // PARTS, block.stop - block.start
+            )
+            if live is None:
+                live = wide_rows[:, 0:1].astype(jnp.float32) < EMPTY_LIMIT
+                wide_rows = jnp.where(live, wide_rows.astype(jnp.float32), 0.0).astype(jnp.bfloat16)
+            rows_ref[rows, block] = wide_rows
+            centred_ref[rows, block] = (wide_rows.astype(jnp.float32) - centre[:, block]).astype(
+                jnp.bfloat16
+            )
+        live_mask = live.astype(jnp.float32)
+        logits = lax.dot_general(
+            rows_ref[rows, :], router_rows, NT, preferred_element_type=jnp.float32
+        )[:, 0:1]
+        gating = jax.nn.sigmoid(logits)
+        for block in latent_blocks:
+            preact = (
+                jnp.dot(
+                    centred_ref[rows, :], encoder_ref[:, block], preferred_element_type=jnp.float32
+                )
+                + bias_ref[:, block]
+            )
+            positive = jnp.maximum(preact, 0.0)
+            positive_ref[rows, block] = positive * live_mask
+            latents_ref[rows, block] = (positive * positive).astype(jnp.bfloat16)
+        held.append((rows, owners, live_mask, gating))
     write_out(rows_ref, rows_hbm, side_sems.at[0])
-    live_mask = live.astype(jnp.float32)
-    logits = lax.dot_general(
-        rows_ref[...],
-        jnp.broadcast_to(router_ref[...], (8, features)),
-        NT,
-        preferred_element_type=jnp.float32,
-    )[:, 0:1]
-    gating = jax.nn.sigmoid(logits)
-    for start, width in column_blocks(encoder_ref.shape[1]):
-        block = slice(start, start + width)
-        preact = (
-            jnp.dot(centred_ref[...], encoder_ref[:, block], preferred_element_type=jnp.float32)
-            + bias_ref[:, block]
-        )
-        positive = jnp.maximum(preact, 0.0)
-        positive_ref[:, block] = positive * live_mask
-        latents_ref[:, block] = (positive * positive).astype(jnp.bfloat16)
     write_out(latents_ref, latents_hbm, side_sems.at[1])
     fetch.wait()
-    projected = jnp.zeros((count, 1), jnp.float32)
-    error_sums = []
-    for i, (start, width) in enumerate(column_blocks(features)):
-        block = slice(start, start + width)
-        ungated = jnp.dot(
-            latents_ref[...], decoder_ref[:, block], preferred_element_type=jnp.float32
+    for part, (rows, owners, live_mask, gating) in enumerate(held):
+        projected = jnp.zeros((count // PARTS, 1), jnp.float32)
+        sums = []
+        for block in blocks:
+            ungated = jnp.dot(
+                latents_ref[rows, :], decoder_ref[:, block], preferred_element_type=jnp.float32
+            )
+            rebuilt = centre[:, block] + gating * ungated
+            outgoing_ref[owners, :, block] = rebuilt.astype(jnp.bfloat16).reshape(
+                sources // PARTS, slot_cap, block.stop - block.start
+            )
+            errors = (rows_ref[rows, block].astype(jnp.float32) - rebuilt) * live_mask
+            backward_ref[rows, block] = (-gating * errors).astype(jnp.bfloat16)
+            projected = projected + jnp.sum(errors * ungated, axis=1, keepdims=True)
+            sums.append(jnp.sum(errors, axis=0, keepdims=True))
+        error_sums.append(jnp.concatenate(sums, axis=1))
+        logit_grad_ref[rows, :] = -projected * gating * (1.0 - gating)
+        sums = []
+        for block in latent_blocks:
+            latent_grad = lax.dot_general(
+                backward_ref[rows, :], decoder_ref[block, :], NT, preferred_element_type=jnp.float32
+            )
+            preact_grad = ((latent_grad + sparsity) * 2.0 * positive_ref[rows, block]).astype(
+                jnp.bfloat16
+            )
+            preact_grad_ref[rows, block] = preact_grad
+            sums.append(jnp.sum(preact_grad.astype(jnp.float32), axis=0, keepdims=True))
+        bias_grads.append(jnp.concatenate(sums, axis=1))
+        write_out(
+            outgoing_ref.at[owners, :, 0:features],
+            outgoing_hbm.at[owners, :, 0:features],
+            sems.at[1 + part],
         )
-        rebuilt = centre[:, block] + gating * ungated
-        outgoing_ref[:, :, block] = rebuilt.astype(jnp.bfloat16).reshape(sources, slot_cap, width)
-        write_out(outgoing_ref.at[:, :, block], outgoing_hbm.at[:, :, block], sems.at[1 + i])
-        errors = (rows_ref[:, block].astype(jnp.float32) - rebuilt) * live_mask
-        backward_ref[:, block] = (-gating * errors).astype(jnp.bfloat16)
-        projected = projected + jnp.sum(errors * ungated, axis=1, keepdims=True)
-        error_sums.append(jnp.sum(errors, axis=0, keepdims=True))
     write_out(backward_ref, backward_hbm, side_sems.at[2])
-    logit_grad_ref[...] = -projected * gating * (1.0 - gating)
-    bias_grads = []
-    for start, width in column_blocks(encoder_ref.shape[1]):
-        block = slice(start, start + width)
-        latent_grad = lax.dot_general(
-            backward_ref[...], decoder_ref[block, :], NT, preferred_element_type=jnp.float32
-        )
-        preact_grad = ((latent_grad + sparsity) * 2.0 * positive_ref[:, block]).astype(jnp.bfloat16)
-        preact_grad_ref[:, block] = preact_grad
-        bias_grads.append(jnp.sum(preact_grad.astype(jnp.float32), axis=0, keepdims=True))
     write_out(preact_grad_ref, preact_grad_hbm, side_sems.at[3])
-    bias_grad = jnp.concatenate(bias_grads, axis=1)
+    bias_grad = sum(bias_grads)
     bias_grad_ref[...] = bias_grad
     high = bias_grad.astype(jnp.bfloat16).astype(jnp.float32)
     middle = (bias_grad - high).astype(jnp.bfloat16).astype(jnp.float32)
@@ -222,13 +244,19 @@
         axis=0,
         keepdims=True,
     )
-    centre_part = -jnp.concatenate(error_sums, axis=1) - passed
+    centre_part = -sum(error_sums) - passed
     pieces = [centre_part[:, i * tail : (i + 1) * tail] for i in range(features // tail)]
     pieces += [jnp.zeros((1, tail), jnp.float32)] * (slot_cap - len(pieces))
     outgoing_ref[:, :, features:] = jnp.broadcast_to(
         jnp.concatenate(pieces, axis=0).astype(jnp.bfloat16)[None], (sources, slot_cap, tail)
     )
-    write_out(outgoing_ref.at[:, :, features:], outgoing_hbm.at[:, :, features:], sems.at[0])
+    for i in range(TAIL_COPIES):
+        owners = slice(i * sources // TAIL_COPIES, (i + 1) * sources // TAIL_COPIES)
+        write_out(
+            outgoing_ref.at[owners, :, features:],
+            outgoing_hbm.at[owners, :, features:],
+            sems.at[1 + PARTS + i],
+        )
     for copy in copies:
         copy.wait()
 
@@ -357,7 +385,7 @@
             pltpu.VMEM((latent_count, features), jnp.bfloat16),
             pltpu.VMEM((devices, slot_cap, wide), jnp.bfloat16),
             pltpu.VMEM((count, latent_count), jnp.float32),
-            pltpu.SemaphoreType.DMA((copies,)),
+            pltpu.SemaphoreType.DMA((1 + PARTS + TAIL_COPIES,)),
             pltpu.SemaphoreType.DMA((4,)),
         ],
         compiler_params=pltpu.CompilerParams(vmem_limit_bytes=VMEM_LIMIT),

time: 70.6 us -> 70.5 us (level)
  no operation moved by 1% of the time
where the time goes in v3:
time: 70.5 us; the launch traced here: 70.1 us
  waiting for transfers between devices  31.1 us (44%)
  Pallas kernels  20.2 us (29%)
  starting transfers between devices  15.8 us (22%)
  other arithmetic  1.38 us (2%)
  between operations  0.87 us (1%)
    all_to_all x1, waiting for transfers between devices, per_device(): lax.all_to_all(packed, AXES, split_axis=0, concat_axis=0, tiled=True)  20.4 us
    pallas_call x1, Pallas kernels, per_device(): pl.pallas_call(step_kernel, in_specs=[local] + [hbm] * 10, out_specs=(hbm...  11.2 us
    all_to_all x1, starting transfers between devices, per_device(): lax.all_to_all(packed, AXES, split_axis=0, concat_axis=0, tiled=True)  11.1 us
    all_to_all x1, waiting for transfers between devices, per_device(): lax.all_to_all(outgoing, AXES, split_axis=0, concat_axis=0, tiled=True)  10.8 us
    pallas_call x1, Pallas kernels, per_device(): pl.pallas_call(expert_kernel, in_specs=[local, local, local, local, local...  4.93 us
    all_to_all x1, starting transfers between devices, per_device(): lax.all_to_all(outgoing, AXES, split_axis=0, concat_axis=0, tiled=True)  4.66 us
    pallas_call x1, Pallas kernels, per_device(): pl.pallas_call(pack_kernel, in_specs=[hbm, hbm], out_specs=hbm, out_shape...  2.42 us
  transfers between devices with their start and end apart: 2, of which 2 were waited for; matrix products, arithmetic and copies ran while one was open for 2% of the time, Pallas kernels for 16%

profile of v3, /device:TPU:0, one launch (start us, length us, event | category | flops | bytes accessed | tf_op | source)
XLA Modules:
  0.0 70.1 jit_solution(2372331936735341718)
XLA Ops:
  0.6 2.4 %pack.1 = bf16[128,4,1152]{2,1,0:T(4,128)(2,1)} custom-call(s32[1,256]{1,0:T(1,128)} %bitcast.17, bf16[256,1152]{1,0:T(8,128)(2,1)} %rows_ref.1), custom_call_target="tpu_custom_call" | custom-call | tf_op jit(solution)/shard_map/pack/pallas_call | solution.py:351
  3.1 0.0 copy-start.5
  3.1 0.0 copy-start
  3.1 0.0 copy-start.1
  3.1 0.0 copy-start.2
  3.1 11.1 %all-to-all-start = ((bf16[128,4,1152]{2,1,0:T(4,128)(2,1)}), bf16[128,4,1152]{2,1,0:T(4,128)(2,1)S(1)}, u32[]{:S(2)}, u32[]{:S(2)}) async-start(bf16[128,4,1152]{2,1,0:T(4,128)(2,1)} %pack.1), calls=%async_computation | async-start | bytes 2359296 | tf_op jit(solution)/shard_map/all_to_all | solution.py:365
  14.3 0.0 copy-done.5
  14.3 20.4 %all-to-all-done.arrived_ref = bf16[128,4,1152]{2,1,0:T(4,128)(2,1)S(1)} async-done(((bf16[128,4,1152]{2,1,0:T(4,128)(2,1)}), bf16[128,4,1152]{2,1,0:T(4,128)(2,1)S(1)}, u32[]{:S(2)}, u32[]{:S(2)}) %all-to-all-start) | async-done | bytes 1179680 | tf_op jit(solution)/shard_map/all_to_all | solution.py:365
  34.7 0.0 copy-done
  34.7 0.0 copy-done.1
  34.7 0.0 copy-done.2
  34.7 4.9 %expert.1 = (bf16[128,4,1536]{2,1,0:T(4,128)(2,1)}, bf16[512,1152]{1,0:T(8,128)(2,1)}, bf16[512,512]{1,0:T(8,128)(2,1)}, bf16[512,1152]{1,0:T(8,128)(2,1)}, bf16...) custom-call(bf16[128,4,1152]{2,1,0:T(4,128)(2,1)S(1)} %all-to-all-done.arrived_ref, ...), custom_call_target="tpu_custom_call" | custom-call | tf_op jit(solution)/shard_map/expert/pallas_call | solution.py:366
  39.6 0.0 copy-start.3
  39.6 0.0 copy-start.6
  39.7 0.0 copy-start.7
  39.7 4.7 %all-to-all-start.1 = ((bf16[128,4,1536]{2,1,0:T(4,128)(2,1)}), bf16[128,4,1536]{2,1,0:T(4,128)(2,1)S(1)}, u32[]{:S(2)}, u32[]{:S(2)}) async-start(bf16[128,4,1536]{2,1,0:T(4,128)(2,1)} %get-tuple-element.33), calls=%async_computation.1 | async-start | bytes 3145728 | tf_op jit(solution)/shard_map/all_to_all | solution.py:401
  44.3 0.0 copy-done.3
  44.3 0.3 taken.1.taken_ref
  44.7 0.0 copy-done.6
  44.7 0.0 copy-done.7
  44.7 0.1 convert_reduce_fusion
  44.9 0.0 copy-start.4
  44.9 11.2 %step.1 = (bf16[1152,512]{1,0:T(8,128)(2,1)}, f32[1152,512]{1,0:T(8,128)}, f32[1152,512]{1,0:T(8,128)}, bf16[512,1152]{1,0:T(8,128)(2,1)}, f32[512,1152]{1,0:T(8,128)}, /*index=5*/f32[512,1152]{1,0:T(8,128)}) custom-call(f32[1,1152]{1,0:T(1,128)S(1)} %broadcast_in_dim.29.centre_ref, bf16[512,1152]{1,0:T(8,128)(2,1)} %get-tuple-element.39.refs_0_, ...), custom_call_target="tpu_custom_call" | custom-call | flops 1207959552 | bytes 11796480 | tf_op jit(solution)/shard_map/step/pallas_call | solution.py:413
  56.1 0.0 copy-done.4
  56.1 0.0 copy-start.10
  56.1 0.0 copy-start.11
  56.1 0.0 copy-start.8
  56.1 0.0 copy-start.9
  56.1 0.3 convolution_reduce_fusion
  56.4 0.4 copy-done.10
  56.8 0.0 copy-done.11
  56.8 0.6 divide_subtract_fusion
  57.4 0.0 copy-done.8
  57.4 0.0 copy-done.9
  57.4 0.6 subtract_convert_fusion
  58.0 10.8 %all-to-all-done.1.returned_ref = bf16[128,4,1536]{2,1,0:T(4,128)(2,1)S(1)} async-done(((bf16[128,4,1536]{2,1,0:T(4,128)(2,1)}), bf16[128,4,1536]{2,1,0:T(4,128)(2,1)S(1)}, u32[]{:S(2)}, u32[]{:S(2)}) %all-to-all-start.1) | async-done | bytes 1572896 | tf_op jit(solution)/shard_map/all_to_all | solution.py:401
  68.8 1.3 %unpack.1 = (bf16[256,1152]{1,0:T(8,128)(2,1)}, f32[1152]{0:T(1024)}, f32[1152]{0:T(1024)}, f32[1152]{0:T(1024)}) custom-call(bf16[256,512]{1,0:T(8,128)(2,1)S(1)} %taken.1.taken_ref, bf16[128,4,1536]{2,1,0:T(4,128)(2,1)S(1)} %all-to-all-done.1.returned_ref, f32[1,1152]{1,0:T(1,128)S(1)} %broadcast_in_dim.29.centre_ref, ...), custom_call_target="tpu_custom_call" | custom-call | tf_op jit(solution)/shard_map/unpack/pallas_call | solution.py:435
  (5 shorter events, 0.0 us)
Async XLA Ops:
  3.1 11.2 %copy-start.5 = (f32[1152]{0:T(1024)S(1)}, f32[1152]{0:T(1024)}, u32[]{:S(2)}) copy-start(f32[1152]{0:T(1024)} %param.19) | copy-start | bytes 13828
  3.1 31.6 %copy-start = (bf16[1,1152,512]{2,1,0:T(8,128)(2,1)S(1)}, bf16[1,1152,512]{2,1,0:T(8,128)(2,1)}, u32[]{:S(2)}) copy-start(bf16[1,1152,512]{2,1,0:T(8,128)(2,1)} %param.25) | copy-start | bytes 3538948
  3.1 31.6 %copy-start.1 = (bf16[1,1152]{1,0:T(2,128)(2,1)S(1)}, bf16[1,1152]{1,0:T(2,128)(2,1)}, u32[]{:S(2)}) copy-start(bf16[1,1152]{1,0:T(2,128)(2,1)} %router_ref.1) | copy-start | bytes 6916
  3.1 31.6 %copy-start.2 = (f32[1,512]{1,0:T(1,128)S(1)}, f32[1,512]{1,0:T(1,128)}, u32[]{:S(2)}) copy-start(f32[1,512]{1,0:T(1,128)} %bias_ref.1) | copy-start | bytes 6148
  3.1 31.6 %all-to-all-start = ((bf16[128,4,1152]{2,1,0:T(4,128)(2,1)}), bf16[128,4,1152]{2,1,0:T(4,128)(2,1)S(1)}, u32[]{:S(2)}, u32[]{:S(2)}) async-start(bf16[128,4,1152]{2,1,0:T(4,128)(2,1)} %pack.1), calls=%async_computation | async-start | bytes 2359296 | tf_op jit(solution)/shard_map/all_to_all | solution.py:365
  39.6 4.7 %copy-start.3 = (s32[256,1]{0,1:T(1,128)S(1)}, s32[256,1]{0,1:T(1,128)}, u32[]{:S(2)}) copy-start(s32[256,1]{0,1:T(1,128)} %param.18) | copy-start | bytes 3076
  39.6 5.0 %copy-start.6 = (f32[1152]{0:T(1024)S(1)}, f32[1152]{0:T(1024)}, u32[]{:S(2)}) copy-start(f32[1152]{0:T(1024)} %param.20) | copy-start | bytes 13828
  39.7 5.0 %copy-start.7 = (f32[1152]{0:T(1024)S(1)}, f32[1152]{0:T(1024)}, u32[]{:S(2)}) copy-start(f32[1152]{0:T(1024)} %param.21) | copy-start | bytes 13828
  39.7 29.1 %all-to-all-start.1 = ((bf16[128,4,1536]{2,1,0:T(4,128)(2,1)}), bf16[128,4,1536]{2,1,0:T(4,128)(2,1)S(1)}, u32[]{:S(2)}, u32[]{:S(2)}) async-start(bf16[128,4,1536]{2,1,0:T(4,128)(2,1)} %get-tuple-element.33), calls=%async_computation.1 | async-start | bytes 3145728 | tf_op jit(solution)/shard_map/all_to_all | solution.py:401
  44.9 11.2 %copy-start.4 = (bf16[512,1152]{1,0:T(8,128)(2,1)S(1)}, bf16[512,1152]{1,0:T(8,128)(2,1)}, u32[]{:S(2)}) copy-start(bf16[512,1152]{1,0:T(8,128)(2,1)} %get-tuple-element.39.refs_0_) | copy-start | bytes 3538948
  56.1 0.7 copy-start.10
  56.1 0.7 copy-start.11
  56.1 1.3 %copy-start.8 = (f32[1,1152]{1,0:T(1,128)S(1)}, f32[1,1152]{1,0:T(1,128)}, u32[]{:S(2)}) copy-start(f32[1,1152]{1,0:T(1,128)} %param.23) | copy-start | bytes 13828
  56.1 1.3 %copy-start.9 = (f32[1,1152]{1,0:T(1,128)S(1)}, f32[1,1152]{1,0:T(1,128)}, u32[]{:S(2)}) copy-start(f32[1,1152]{1,0:T(1,128)} %param.24) | copy-start | bytes 13828

commit v4 on v2

--- a/solution.py
+++ b/solution.py
@@ -19,6 +19,7 @@
 EMPTY_LIMIT = 32.0
 VMEM_LIMIT = 20 * 1024 * 1024
 STEP_LIMIT = 36 * 1024 * 1024
+PAIR = 2
 NT = (((1,), (1,)), ((), ()))
 TN = (((0,), (0,)), ((), ()))
 
@@ -34,6 +35,25 @@
     return (stepped.astype(weights_in.dtype), first_new, second_new)
 
 
+def slot_rows(ref, block, features):
+    devices = ref.shape[0]
+    halves = [
+        ref[:, :, start + block.start : start + block.stop].reshape(
+            devices * PAIR, block.stop - block.start
+        )
+        for start in (0, features)
+    ]
+    return jnp.concatenate(halves, axis=0)
+
+
+def put_slot_rows(ref, block, features, values):
+    devices = ref.shape[0]
+    for i, start in enumerate((0, features)):
+        ref[:, :, start + block.start : start + block.stop] = values[
+            i * devices * PAIR : (i + 1) * devices * PAIR
+        ].reshape(devices, PAIR, block.stop - block.start)
+
+
 def slot_matrix(route_row, experts, slot_cap):
     rows = route_row.shape[1]
     onehot = lax.broadcasted_iota(jnp.int32, (experts, rows), 0) == route_row
@@ -47,7 +67,8 @@
         preferred_element_type=jnp.float32,
     )
     rank = jnp.sum(before * onehot, axis=0, keepdims=True).astype(jnp.int32)
-    position = route_row * slot_cap + rank
+    late = rank >= PAIR
+    position = route_row * PAIR + jnp.where(late, rank - PAIR + experts * PAIR, rank)
     chosen = lax.broadcasted_iota(jnp.int32, (experts * slot_cap, rows), 0) == position
     return chosen.astype(jnp.float32)
 
@@ -59,7 +80,8 @@
 
 
 def pack_kernel(route_ref, rows_ref, packed_ref, route_vmem, rows_vmem, packed_vmem, sems):
-    experts, slot_cap, features = packed_ref.shape
+    experts, features = packed_ref.shape[0], rows_ref.shape[1]
+    slot_cap = packed_ref.shape[2] // features * PAIR
     fetch_route = pltpu.make_async_copy(route_ref, route_vmem, sems.at[1])
     fetch_route.start()
     fetch = pltpu.make_async_copy(rows_ref, rows_vmem, sems.at[0])
@@ -70,18 +92,24 @@
     chosen = chosen.astype(jnp.bfloat16)
     fetch.wait()
     copies = []
-    for i, (start, width) in enumerate(column_blocks(features)):
+    ends = (3 * column_blocks(features)[0][1], features)
+    for start, width in column_blocks(features):
         block = slice(start, start + width)
         part = jnp.dot(chosen, rows_vmem[:, block], preferred_element_type=jnp.float32)
         if start == 0:
             part = part + mark
-        packed_vmem[:, :, block] = part.astype(jnp.bfloat16).reshape(experts, slot_cap, width)
-        copies.append(
-            pltpu.make_async_copy(
-                packed_vmem.at[:, :, block], packed_ref.at[:, :, block], sems.at[1 + i]
+        put_slot_rows(packed_vmem, block, features, part.astype(jnp.bfloat16))
+        if start + width not in ends:
+            continue
+        ready = max((end for end in ends if end <= start), default=0)
+        for shift in (0, features):
+            place = slice(shift + ready, shift + start + width)
+            copies.append(
+                pltpu.make_async_copy(
+                    packed_vmem.at[:, :, place], packed_ref.at[:, :, place], sems.at[2 + len(copies)]
+                )
             )
-        )
-        copies[-1].start()
+            copies[-1].start()
     for copy in copies:
         copy.wait()
 
@@ -90,24 +118,23 @@
     taken_ref, returned_ref, centre_ref, first_ref, second_ref,
     recon_ref, new_centre_ref, new_first_ref, new_second_ref,
 ):
-    experts, slot_cap, wide = returned_ref.shape
     features = recon_ref.shape[1]
-    tail = wide - features
+    tail = returned_ref.shape[2] - 2 * features
     taken = taken_ref[...]
     for start, width in column_blocks(features):
         block = slice(start, start + width)
-        returned = returned_ref[:, :, block].reshape(experts * slot_cap, width)
         recon_ref[:, block] = jnp.dot(
-            taken, returned, preferred_element_type=jnp.float32
+            taken, slot_rows(returned_ref, block, features), preferred_element_type=jnp.float32
         ).astype(jnp.bfloat16)
-    total = jnp.sum(returned_ref[:, :, features:].astype(jnp.float32), axis=0)
-    for i in range(features // tail):
-        block = slice(i * tail, (i + 1) * tail)
+    total = jnp.sum(returned_ref[:, :, 2 * features :].astype(jnp.float32), axis=0)
+    for i in range(PAIR):
+        block = slice(i * tail, min((i + 1) * tail, features))
+        width = block.stop - block.start
         updated = adam_update(
-            centre_ref[:, block], total[i : i + 1], first_ref[:, block], second_ref[:, block]
+            centre_ref[:, block], total[i : i + 1, :width], first_ref[:, block], second_ref[:, block]
         )
         for value, target in zip(updated, (new_centre_ref, new_first_ref, new_second_ref)):
-            target[block] = value.reshape(tail)
+            target[block] = value.reshape(width)
 
 
 def column_blocks(features, width=256):
@@ -139,9 +166,9 @@
     sems,
     side_sems,
 ):
-    sources, slot_cap, features = arrived_ref.shape
-    count = sources * slot_cap
-    tail = outgoing_ref.shape[2] - features
+    sources, features = arrived_ref.shape[0], rows_ref.shape[1]
+    count = rows_ref.shape[0]
+    tail = outgoing_ref.shape[2] - 2 * features
     fetch = pltpu.make_async_copy(decoder_hbm, decoder_ref, sems.at[0])
     fetch.start()
     copies = []
@@ -154,7 +181,7 @@
     live = None
     for start, width in column_blocks(features):
         block = slice(start, start + width)
-        wide_rows = arrived_ref[:, :, block].reshape(count, width)
+        wide_rows = slot_rows(arrived_ref, block, features)
         if live is None:
             live = wide_rows[:, 0:1].astype(jnp.float32) < EMPTY_LIMIT
             wide_rows = jnp.where(live, wide_rows.astype(jnp.float32), 0.0).astype(jnp.bfloat16)
@@ -184,18 +211,19 @@
     fetch.wait()
     projected = jnp.zeros((count, 1), jnp.float32)
     error_sums = []
-    for i, (start, width) in enumerate(column_blocks(features)):
+    for start, width in column_blocks(features):
         block = slice(start, start + width)
         ungated = jnp.dot(
             latents_ref[...], decoder_ref[:, block], preferred_element_type=jnp.float32
         )
         rebuilt = centre[:, block] + gating * ungated
-        outgoing_ref[:, :, block] = rebuilt.astype(jnp.bfloat16).reshape(sources, slot_cap, width)
-        write_out(outgoing_ref.at[:, :, block], outgoing_hbm.at[:, :, block], sems.at[1 + i])
+        put_slot_rows(outgoing_ref, block, features, rebuilt.astype(jnp.bfloat16))
         errors = (rows_ref[:, block].astype(jnp.float32) - rebuilt) * live_mask
         backward_ref[:, block] = (-gating * errors).astype(jnp.bfloat16)
         projected = projected + jnp.sum(errors * ungated, axis=1, keepdims=True)
         error_sums.append(jnp.sum(errors, axis=0, keepdims=True))
+    body = slice(0, 2 * features)
+    write_out(outgoing_ref.at[:, :, body], outgoing_hbm.at[:, :, body], sems.at[1])
     write_out(backward_ref, backward_hbm, side_sems.at[2])
     logit_grad_ref[...] = -projected * gating * (1.0 - gating)
     bias_grads = []
@@ -223,12 +251,15 @@
         keepdims=True,
     )
     centre_part = -jnp.concatenate(error_sums, axis=1) - passed
-    pieces = [centre_part[:, i * tail : (i + 1) * tail] for i in range(features // tail)]
-    pieces += [jnp.zeros((1, tail), jnp.float32)] * (slot_cap - len(pieces))
-    outgoing_ref[:, :, features:] = jnp.broadcast_to(
-        jnp.concatenate(pieces, axis=0).astype(jnp.bfloat16)[None], (sources, slot_cap, tail)
-    )
-    write_out(outgoing_ref.at[:, :, features:], outgoing_hbm.at[:, :, features:], sems.at[0])
+    spare = jnp.zeros((1, PAIR * tail - features), jnp.float32)
+    padded = jnp.concatenate([centre_part, spare], axis=1)
+    pieces = [padded[:, i * tail : (i + 1) * tail] for i in range(PAIR)]
+    outgoing_ref[:, :, 2 * features :] = jnp.broadcast_to(
+        jnp.concatenate(pieces, axis=0).astype(jnp.bfloat16)[None], (sources, PAIR, tail)
+    )
+    write_out(
+        outgoing_ref.at[:, :, 2 * features :], outgoing_hbm.at[:, :, 2 * features :], sems.at[0]
+    )
     for copy in copies:
         copy.wait()
 
@@ -314,21 +345,21 @@
     latent_count = encoder.shape[2]
     slot_cap = 2 * row_count // devices
     count = devices * slot_cap
-    wide = features + features // (slot_cap - 1)
+    wide = 2 * features + -(-features // (128 * PAIR)) * 128
     params = pltpu.CompilerParams(vmem_limit_bytes=VMEM_LIMIT)
     hbm = pl.BlockSpec(memory_space=pltpu.HBM)
     local = pl.BlockSpec(memory_space=pltpu.VMEM)
-    copies = len(column_blocks(features)) + 1
+    copies = 2 * len(column_blocks(features)) + 2
     route_row = routes.reshape(1, row_count)
     packed = pl.pallas_call(
         pack_kernel,
         in_specs=[hbm, hbm],
         out_specs=hbm,
-        out_shape=pltpu.HBM((devices, slot_cap, features), jnp.bfloat16),
+        out_shape=pltpu.HBM((devices, PAIR, 2 * features), jnp.bfloat16),
         scratch_shapes=[
             pltpu.VMEM((1, row_count), jnp.int32),
             pltpu.VMEM((row_count, features), jnp.bfloat16),
-            pltpu.VMEM((devices, slot_cap, features), jnp.bfloat16),
+            pltpu.VMEM((devices, PAIR, 2 * features), jnp.bfloat16),
             pltpu.SemaphoreType.DMA((copies,)),
         ],
         compiler_params=pltpu.CompilerParams(vmem_limit_bytes=VMEM_LIMIT),
@@ -340,7 +371,7 @@
         in_specs=[local, local, local, local, local, hbm],
         out_specs=(hbm,) * 5 + (local,) * 2,
         out_shape=(
-            pltpu.HBM((devices, slot_cap, wide), jnp.bfloat16),
+            pltpu.HBM((devices, PAIR, wide), jnp.bfloat16),
             pltpu.HBM((count, features), jnp.bfloat16),
             pltpu.HBM((count, latent_count), jnp.bfloat16),
             pltpu.HBM((count, features), jnp.bfloat16),
@@ -355,7 +386,7 @@
             pltpu.VMEM((count, latent_count), jnp.bfloat16),
             pltpu.VMEM((count, features), jnp.bfloat16),
             pltpu.VMEM((latent_count, features), jnp.bfloat16),
-            pltpu.VMEM((devices, slot_cap, wide), jnp.bfloat16),
+            pltpu.VMEM((devices, PAIR, wide), jnp.bfloat16),
             pltpu.VMEM((count, latent_count), jnp.float32),
             pltpu.SemaphoreType.DMA((copies,)),
             pltpu.SemaphoreType.DMA((4,)),

time: 70.6 us -> 70.5 us (level)
  waiting for transfers between devices: 31.1 us -> 30.3 us
    all_to_all x1, waiting for transfers between devices: 10.8 us -> 9.91 us  [per_device(): lax.all_to_all(outgoing, AXES, split_axis=0, concat_axis=0, tiled=True)]
where the time goes in v4:
time: 70.5 us; the launch traced here: 70.2 us
  waiting for transfers between devices  30.3 us (43%)
  Pallas kernels  20.9 us (30%)
  starting transfers between devices  16 us (23%)
  other arithmetic  1.38 us (2%)
  between operations  0.87 us (1%)
    all_to_all x1, waiting for transfers between devices, per_device(): lax.all_to_all(packed, AXES, split_axis=0, concat_axis=0, tiled=True)  20.4 us
    pallas_call x1, Pallas kernels, per_device(): pl.pallas_call(step_kernel, in_specs=[local] + [hbm] * 10, out_specs=(hbm...  11.2 us
    all_to_all x1, starting transfers between devices, per_device(): lax.all_to_all(packed, AXES, split_axis=0, concat_axis=0, tiled=True)  11.1 us
    all_to_all x1, waiting for transfers between devices, per_device(): lax.all_to_all(outgoing, AXES, split_axis=0, concat_axis=0, tiled=True)  9.91 us
    pallas_call x1, Pallas kernels, per_device(): pl.pallas_call(expert_kernel, in_specs=[local, local, local, local, local...  5.28 us
    all_to_all x1, starting transfers between devices, per_device(): lax.all_to_all(outgoing, AXES, split_axis=0, concat_axis=0, tiled=True)  4.84 us
    pallas_call x1, Pallas kernels, per_device(): pl.pallas_call(pack_kernel, in_specs=[hbm, hbm], out_specs=hbm, out_shape...  2.62 us
    pallas_call x1, Pallas kernels, per_device(): pl.pallas_call(unpack_kernel, out_shape=(jax.ShapeDtypeStruct((row_count,...  1.5 us
  transfers between devices with their start and end apart: 2, of which 2 were waited for; matrix products, arithmetic and copies ran while one was open for 2% of the time, Pallas kernels for 16%

profile of v4, /device:TPU:0, one launch (start us, length us, event | category | flops | bytes accessed | tf_op | source)
XLA Modules:
  0.0 70.2 jit_solution(17757893120133095397)
XLA Ops:
  0.6 2.6 %pack.1 = bf16[128,2,2304]{2,1,0:T(2,128)(2,1)} custom-call(s32[1,256]{1,0:T(1,128)} %bitcast.17, bf16[256,1152]{1,0:T(8,128)(2,1)} %rows_ref.1), custom_call_target="tpu_custom_call" | custom-call | tf_op jit(solution)/shard_map/pack/pallas_call | solution.py:354
  3.3 0.0 copy-start.5
  3.3 0.0 copy-start
  3.3 0.0 copy-start.1
  3.3 0.0 copy-start.2
  3.3 11.1 %all-to-all-start = ((bf16[128,2,2304]{2,1,0:T(2,128)(2,1)}), bf16[128,2,2304]{2,1,0:T(2,128)(2,1)S(1)}, u32[]{:S(2)}, u32[]{:S(2)}) async-start(bf16[128,2,2304]{2,1,0:T(2,128)(2,1)} %pack.1), calls=%async_computation | async-start | bytes 2359296 | tf_op jit(solution)/shard_map/all_to_all | solution.py:368
  14.5 0.0 copy-done.5
  14.5 20.4 %all-to-all-done.arrived_ref = bf16[128,2,2304]{2,1,0:T(2,128)(2,1)S(1)} async-done(((bf16[128,2,2304]{2,1,0:T(2,128)(2,1)}), bf16[128,2,2304]{2,1,0:T(2,128)(2,1)S(1)}, u32[]{:S(2)}, u32[]{:S(2)}) %all-to-all-start) | async-done | bytes 1179680 | tf_op jit(solution)/shard_map/all_to_all | solution.py:368
  34.9 0.0 copy-done
  34.9 0.0 copy-done.1
  34.9 0.0 copy-done.2
  34.9 5.3 %expert.1 = (bf16[128,2,2944]{2,1,0:T(2,128)(2,1)}, bf16[512,1152]{1,0:T(8,128)(2,1)}, bf16[512,512]{1,0:T(8,128)(2,1)}, bf16[512,1152]{1,0:T(8,128)(2,1)}, bf16...) custom-call(bf16[128,2,2304]{2,1,0:T(2,128)(2,1)S(1)} %all-to-all-done.arrived_ref, ...), custom_call_target="tpu_custom_call" | custom-call | tf_op jit(solution)/shard_map/expert/pallas_call | solution.py:369
  40.2 0.0 copy-start.3
  40.2 0.0 copy-start.6
  40.2 0.0 copy-start.7
  40.2 4.8 %all-to-all-start.1 = ((bf16[128,2,2944]{2,1,0:T(2,128)(2,1)}), bf16[128,2,2944]{2,1,0:T(2,128)(2,1)S(1)}, u32[]{:S(2)}, u32[]{:S(2)}) async-start(bf16[128,2,2944]{2,1,0:T(2,128)(2,1)} %get-tuple-element.33), calls=%async_computation.1 | async-start | bytes 3014656 | tf_op jit(solution)/shard_map/all_to_all | solution.py:404
  45.1 0.0 copy-done.3
  45.1 0.3 taken.1.taken_ref
  45.4 0.0 copy-done.6
  45.4 0.0 copy-done.7
  45.5 0.1 convert_reduce_fusion
  45.6 0.0 copy-start.4
  45.6 11.2 %step.1 = (bf16[1152,512]{1,0:T(8,128)(2,1)}, f32[1152,512]{1,0:T(8,128)}, f32[1152,512]{1,0:T(8,128)}, bf16[512,1152]{1,0:T(8,128)(2,1)}, f32[512,1152]{1,0:T(8,128)}, /*index=5*/f32[512,1152]{1,0:T(8,128)}) custom-call(f32[1,1152]{1,0:T(1,128)S(1)} %broadcast_in_dim.29.centre_ref, bf16[512,1152]{1,0:T(8,128)(2,1)} %get-tuple-element.39.refs_0_, ...), custom_call_target="tpu_custom_call" | custom-call | flops 1207959552 | bytes 11796480 | tf_op jit(solution)/shard_map/step/pallas_call | solution.py:416
  56.8 0.0 copy-done.4
  56.8 0.0 copy-start.10
  56.8 0.0 copy-start.11
  56.8 0.0 copy-start.8
  56.9 0.0 copy-start.9
  56.9 0.3 convolution_reduce_fusion
  57.1 0.4 copy-done.10
  57.5 0.0 copy-done.11
  57.5 0.6 divide_subtract_fusion
  58.1 0.0 copy-done.8
  58.1 0.0 copy-done.9
  58.1 0.6 subtract_convert_fusion
  58.8 9.9 %all-to-all-done.1.returned_ref = bf16[128,2,2944]{2,1,0:T(2,128)(2,1)S(1)} async-done(((bf16[128,2,2944]{2,1,0:T(2,128)(2,1)}), bf16[128,2,2944]{2,1,0:T(2,128)(2,1)S(1)}, u32[]{:S(2)}, u32[]{:S(2)}) %all-to-all-start.1) | async-done | bytes 1507360 | tf_op jit(solution)/shard_map/all_to_all | solution.py:404
  68.7 1.5 %unpack.1 = (bf16[256,1152]{1,0:T(8,128)(2,1)}, f32[1152]{0:T(1024)}, f32[1152]{0:T(1024)}, f32[1152]{0:T(1024)}) custom-call(bf16[256,512]{1,0:T(8,128)(2,1)S(1)} %taken.1.taken_ref, bf16[128,2,2944]{2,1,0:T(2,128)(2,1)S(1)} %all-to-all-done.1.returned_ref, f32[1,1152]{1,0:T(1,128)S(1)} %broadcast_in_dim.29.centre_ref, ...), custom_call_target="tpu_custom_call" | custom-call | tf_op jit(solution)/shard_map/unpack/pallas_call | solution.py:438
  (5 shorter events, 0.0 us)
Async XLA Ops:
  3.3 11.2 %copy-start.5 = (f32[1152]{0:T(1024)S(1)}, f32[1152]{0:T(1024)}, u32[]{:S(2)}) copy-start(f32[1152]{0:T(1024)} %param.19) | copy-start | bytes 13828
  3.3 31.6 %copy-start = (bf16[1,1152,512]{2,1,0:T(8,128)(2,1)S(1)}, bf16[1,1152,512]{2,1,0:T(8,128)(2,1)}, u32[]{:S(2)}) copy-start(bf16[1,1152,512]{2,1,0:T(8,128)(2,1)} %param.25) | copy-start | bytes 3538948
  3.3 31.6 %copy-start.1 = (bf16[1,1152]{1,0:T(2,128)(2,1)S(1)}, bf16[1,1152]{1,0:T(2,128)(2,1)}, u32[]{:S(2)}) copy-start(bf16[1,1152]{1,0:T(2,128)(2,1)} %router_ref.1) | copy-start | bytes 6916
  3.3 31.6 %copy-start.2 = (f32[1,512]{1,0:T(1,128)S(1)}, f32[1,512]{1,0:T(1,128)}, u32[]{:S(2)}) copy-start(f32[1,512]{1,0:T(1,128)} %bias_ref.1) | copy-start | bytes 6148
  3.3 31.6 %all-to-all-start = ((bf16[128,2,2304]{2,1,0:T(2,128)(2,1)}), bf16[128,2,2304]{2,1,0:T(2,128)(2,1)S(1)}, u32[]{:S(2)}, u32[]{:S(2)}) async-start(bf16[128,2,2304]{2,1,0:T(2,128)(2,1)} %pack.1), calls=%async_computation | async-start | bytes 2359296 | tf_op jit(solution)/shard_map/all_to_all | solution.py:368
  40.2 4.9 %copy-start.3 = (s32[256,1]{0,1:T(1,128)S(1)}, s32[256,1]{0,1:T(1,128)}, u32[]{:S(2)}) copy-start(s32[256,1]{0,1:T(1,128)} %param.18) | copy-start | bytes 3076
  40.2 5.2 %copy-start.6 = (f32[1152]{0:T(1024)S(1)}, f32[1152]{0:T(1024)}, u32[]{:S(2)}) copy-start(f32[1152]{0:T(1024)} %param.20) | copy-start | bytes 13828
  40.2 5.2 %copy-start.7 = (f32[1152]{0:T(1024)S(1)}, f32[1152]{0:T(1024)}, u32[]{:S(2)}) copy-start(f32[1152]{0:T(1024)} %param.21) | copy-start | bytes 13828
  40.2 28.5 %all-to-all-start.1 = ((bf16[128,2,2944]{2,1,0:T(2,128)(2,1)}), bf16[128,2,2944]{2,1,0:T(2,128)(2,1)S(1)}, u32[]{:S(2)}, u32[]{:S(2)}) async-start(bf16[128,2,2944]{2,1,0:T(2,128)(2,1)} %get-tuple-element.33), calls=%async_computation.1 | async-start | bytes 3014656 | tf_op jit(solution)/shard_map/all_to_all | solution.py:404
  45.6 11.2 %copy-start.4 = (bf16[512,1152]{1,0:T(8,128)(2,1)S(1)}, bf16[512,1152]{1,0:T(8,128)(2,1)}, u32[]{:S(2)}) copy-start(bf16[512,1152]{1,0:T(8,128)(2,1)} %get-tuple-element.39.refs_0_) | copy-start | bytes 3538948
  56.8 0.7 copy-start.10
  56.8 0.7 copy-start.11
  56.8 1.3 %copy-start.8 = (f32[1,1152]{1,0:T(1,128)S(1)}, f32[1,1152]{1,0:T(1,128)}, u32[]{:S(2)}) copy-start(f32[1,1152]{1,0:T(1,128)} %param.23) | copy-start | bytes 13828
  56.9 1.3 %copy-start.9 = (f32[1,1152]{1,0:T(1,128)S(1)}, f32[1,1152]{1,0:T(1,128)}, u32[]{:S(2)}) copy-start(f32[1,1152]{1,0:T(1,128)} %param.24) | copy-start | bytes 13828
